TPU v7x, 32 devices: a whole 2x2x4 slice. The times are simulated.
32 devices in a mesh: section: 2 (over x), expert: 4 (over y, core), dp: 4 (over z).
Axes of the slice: x: 2, y: 2, z: 4, core: 2. Of those that a mesh axis runs over, the one named last changes fastest.
Arguments:
- tokens: bfloat16 [512, 3072], P('expert', 'dp'), may hold values from -6 to 6
- expert_ids: int32 [512, 2], P('expert'), may hold values from 0 to 3, all different within a row; in each aligned block of 128 rows (0 to 127, 128 to 255, ...) at most 128 rows name the same one
- w_gate: bfloat16 [4, 3072, 8192], P('expert', 'dp', 'section'), may hold values from -0.109375 to 0.109375
- w_up: bfloat16 [4, 3072, 8192], P('expert', 'dp', 'section'), may hold values from -0.109375 to 0.109375
- cotangent: bfloat16 [4, 512, 8192], P('expert', None, 'section'), may hold values from -6 to 6
Outputs:
- acted: bfloat16 [4, 512, 8192], P('expert', None, 'section')
- input_grad: bfloat16 [512, 3072], P('expert', 'dp')
- gate_grad: bfloat16 [4, 3072, 8192], P('expert', 'dp', 'section')
- up_grad: bfloat16 [4, 3072, 8192], P('expert', 'dp', 'section')
Inputs may be any that keep to these rules, and one draw needn't show every extreme that they name: `expert_ids`: each token names two different experts. Among the 128 tokens of one index of the expert axis no expert is named more than 128 times, a bound that some block reaches.
All inputs are finite; a program needn't handle non-finite values.
Results may differ from a plain program's by a relative error of at most 0.0049.
Values may be sent and summed in bfloat16 or wider, within the bound.
No kernel may reach another device: no remote copies, remote signals or barrier semaphores. Data moves between devices by JAX's collectives and lax.ppermute only.
A program may use at most 128 MiB of HBM per device.

v0:
```python
import jax
import jax.numpy as jnp
from jax import lax
from jax.sharding import PartitionSpec as P


def local(tokens, expert_ids, w_gate, w_up, cotangent):
    rows, width = tokens.shape
    experts = lax.axis_size("expert")
    capacity = min(rows, 4 * rows // experts)
    wg = w_gate[0]
    wu = w_up[0]
    flat_ids = expert_ids.reshape(-1)
    member = (flat_ids[:, None] == jnp.arange(experts, dtype=jnp.int32)[None, :]).astype(jnp.int32)
    rank = jnp.sum((jnp.cumsum(member, axis=0) - member) * member, axis=1)
    slot = flat_ids * capacity + rank
    token_of = jnp.arange(2 * rows, dtype=jnp.int32) // 2
    source = jnp.full((experts * capacity,), rows, jnp.int32).at[slot].set(token_of)
    occupied = jnp.zeros((experts * capacity,), jnp.bfloat16).at[slot].set(1.0)
    x_pad = jnp.concatenate([tokens, jnp.zeros((1, width), jnp.bfloat16)], axis=0)
    send_x = jnp.take(x_pad, source, axis=0).reshape(experts, capacity, width)
    recv_x, recv_live = (
        lax.all_to_all(send_x, "expert", split_axis=0, concat_axis=0, tiled=True),
        lax.all_to_all(
            occupied.reshape(experts, capacity), "expert", split_axis=0, concat_axis=0, tiled=True
        ),
    )
    x_rows = recv_x.reshape(-1, width)
    parts = (x_rows,)
    part_gate = jnp.dot(parts[0], wg, preferred_element_type=jnp.float32)
    part_up = jnp.dot(parts[0], wu, preferred_element_type=jnp.float32)
    pre_gate, pre_up = lax.psum((part_gate, part_up), "dp")
    sig = jax.nn.sigmoid(pre_gate)
    silu_v = pre_gate * sig
    acted = (silu_v * pre_up).astype(jnp.bfloat16)
    cf = cotangent[0].astype(jnp.float32)
    gate_part = (cf * pre_up * sig * (1.0 + pre_gate * (1.0 - sig))).astype(jnp.bfloat16)
    up_part = (cf * silu_v).astype(jnp.bfloat16)
    contract = (((0,), (0,)), ((), ()))
    gate_grad = lax.dot_general(x_rows, gate_part, contract, preferred_element_type=jnp.float32)
    up_grad = lax.dot_general(x_rows, up_part, contract, preferred_element_type=jnp.float32)
    parts = (gate_part, up_part)
    back = lax.dot_general(
        parts[0], wg, (((1,), (1,)), ((), ())), preferred_element_type=jnp.float32
    ) + lax.dot_general(parts[1], wu, (((1,), (1,)), ((), ())), preferred_element_type=jnp.float32)
    back = (back,)[0]
    whole = lax.psum(back, "section")
    home = lax.all_to_all(
        whole.reshape(experts, capacity, width), "expert", split_axis=0, concat_axis=0, tiled=True
    )
    token_grad = jnp.sum(
        jnp.take(home.reshape(-1, width), slot, axis=0).reshape(rows, 2, width), axis=1
    )
    return (
        acted[None],
        token_grad.astype(jnp.bfloat16),
        gate_grad.astype(jnp.bfloat16)[None],
        up_grad.astype(jnp.bfloat16)[None],
    )


def solution(mesh):
    placed = (
        P("expert", "dp"),
        P("expert", None),
        P("expert", "dp", "section"),
        P("expert", "dp", "section"),
        P("expert", None, "section"),
    )
    return jax.shard_map(
        local,
        mesh=mesh,
        in_specs=placed,
        out_specs=(
            P("expert", None, "section"),
            P("expert", "dp"),
            P("expert", "dp", "section"),
            P("expert", "dp", "section"),
        ),
        check_vma=False,
    )
```

profile of v0, /device:TPU:0, one launch (start us, length us, event | category | flops | bytes accessed | tf_op | source)
XLA Modules:
  0.0 716.1 jit_solution(4372841269504574821)
XLA Ops:
  7.2 0.8 copy.18
  8.3 0.7 broadcast_multiply_fusion
  9.0 1.2 reduce-window.6
  10.7 0.1 mul.45
  10.9 1.4 scatter_custom_fusion
  12.3 0.9 concatenate.3
  13.3 2.0 gather_fusion
  15.3 0.1 broadcast_select_fusion
  15.5 16.0 %all_to_all.10 = bf16[4,128,768]{2,1,0:T(8,128)(2,1)S(1)} all-to-all(bf16[4,128,768]{2,1,0:T(8,128)(2,1)S(1)} %broadcast_select_fusion), channel_id=1, replica_groups=mesh['section'=2,'expert'=4,'dp'=4] {'expert'}, dimensions={0} | all-to-all | bytes 1572864 | tf_op jit(solution)/shard_map/all_to_all | solution.py:23
  31.4 8.5 %fusion.11 = f32[512,4096]{1,0:T(8,128)} fusion(bf16[512,768]{1,0:T(8,128)(2,1)S(1)} %bitcast.58, bf16[1,768,4096]{2,1,0:T(8,128)(2,1)} %param.7), kind=kOutput, calls=%fused_computation.20 | convolution fusion | flops 3221225472 | bytes 15466496 | tf_op jit(solution)/shard_map/dot_general | solution.py:30
  39.9 5.6 fusion.7
  45.5 0.2 all-reduce.5.cloned.1.call-start
  45.7 563.5 %all-reduce.7.cloned.1.call-done = (f32[512,4096]{1,0:T(8,128)}, f32[512,4096]{1,0:T(8,128)}) async-done(((f32[512,4096]{1,0:T(8,128)}, f32[512,4096]{1,0:T(8,128)}), (f32[512,4096]{1,0:T(8,128)}, f32[512,4096]{1,0:T(8,128)})) %all-reduce.7.cloned.1.call-update) | async-done | bytes 16777232 | tf_op jit(solution)/shard_map/psum | solution.py:32
  609.2 11.5 %fusion.2 = (bf16[512,4096]{1,0:T(8,128)(2,1)S(1)}, bf16[1,512,4096]{2,1,0:T(8,128)(2,1)}, bf16[512,4096]{1,0:T(8,128)(2,1)S(1)}) fusion(f32[512,4096]{1,0:T(8,128)} %get-tuple-element.4, f32[512,4096]{1,0:T(8,128)} %get-tuple-element.5, bf16[1,512,4096]{2,1,0:T(8,128)(2,1)} %param.9), kind=kLoop, calls=%fused_computation.7 | loop fusion | flops 33554432 | bytes 33554432 | tf_op jit(solution)/shard_map/convert_element_type | solution.py:37
  620.7 3.5 fusion.5
  624.2 7.4 %fusion.16 = f32[512,768]{1,0:T(8,128)} fusion(f32[512,768]{1,0:T(8,128)S(1)} %fusion.5, bf16[512,4096]{1,0:T(8,128)(2,1)S(1)} %get-tuple-element.6, bf16[1,768,4096]{2,1,0:T(8,128)(2,1)} %param.7), kind=kOutput, calls=%fused_computation.25 | convolution fusion | flops 3221618688 | bytes 13631488 | tf_op jit(solution)/shard_map/dot_general | solution.py:43
  632.0 50.3 %all-reduce.5.cloned.1.call-done = f32[4,128,768]{2,1,0:T(8,128)} async-done(((f32[4,128,768]{2,1,0:T(8,128)}), f32[4,128,768]{2,1,0:T(8,128)}) %all-reduce.5.cloned.1.call-update) | async-done | bytes 1572880 | tf_op jit(solution)/shard_map/psum | solution.py:47
  682.3 3.8 all-to-all-start.1
  686.1 7.7 %fusion.13 = bf16[1,768,4096]{2,1,0:T(8,128)(2,1)} fusion(bf16[512,768]{1,0:T(8,128)(2,1)S(1)} %bitcast.60, bf16[512,4096]{1,0:T(8,128)(2,1)} %copy-done.2), kind=kOutput, calls=%fused_computation.22 | convolution fusion | flops 3224371200 | bytes 11272192 | tf_op jit(solution)/shard_map/dot_general | solution.py:40
  693.8 5.4 fusion.14
  699.2 6.7 all-to-all-done.1
  705.9 1.1 gather_fusion.1
  707.0 0.5 gather.15
  707.5 1.8 select_reduce_fusion
  (42 shorter events, 1.3 us)
Async XLA Ops:
  7.2 602.0 %all-reduce.7.cloned.1.call-start = ((), (), s32[]{:S(2)}) async-start(), calls=%async_computation.3 | async-start | bytes 33554432 | tf_op jit(solution)/shard_map/psum | solution.py:32
  15.4 24.5 %slice-start = ((s8[6291456]{0:T(1024)(128)(4,1)}), s8[4194304]{0:T(1024)(128)(4,1)S(1)}, s32[]{:S(2)}) async-start(s8[6291456]{0:T(1024)(128)(4,1)} %bitcast.62), calls=%async_computation.4 | async-start | bytes 8388608
  31.4 8.5 %slice-start.1 = ((s8[6291456]{0:T(1024)(128)(4,1)}), s8[2097152]{0:T(1024)(128)(4,1)S(1)}, s32[]{:S(2)}) async-start(s8[6291456]{0:T(1024)(128)(4,1)} %bitcast.62), calls=%async_computation.5 | async-start | bytes 4194304
  45.5 575.2 %slice-start.2 = ((s8[6291456]{0:T(1024)(128)(4,1)}), s8[2097152]{0:T(1024)(128)(4,1)S(1)}, s32[]{:S(2)}) async-start(s8[6291456]{0:T(1024)(128)(4,1)} %bitcast.64), calls=%async_computation.6 | async-start | bytes 4194304
  45.5 636.8 %all-reduce.5.cloned.1.call-start = ((), (), s32[]{:S(2)}) async-start(), calls=%async_computation.2 | async-start | bytes 3145728 | tf_op jit(solution)/shard_map/psum | solution.py:47
  609.2 11.5 %slice-start.3 = ((s8[6291456]{0:T(1024)(128)(4,1)}), s8[4194304]{0:T(1024)(128)(4,1)S(1)}, s32[]{:S(2)}) async-start(s8[6291456]{0:T(1024)(128)(4,1)} %bitcast.64), calls=%async_computation.7 | async-start | bytes 8388608
  620.7 3.5 copy-start
  620.7 3.5 copy-start.2
  624.2 7.6 %copy-start.3 = (s32[128,2]{0,1:T(2,128)S(1)}, s32[128,2]{0,1:T(2,128)}, u32[]{:S(2)}) copy-start(s32[128,2]{0,1:T(2,128)} %param.6) | copy-start | bytes 3076
  682.3 23.6 %all-to-all-start.1 = ((f32[4,128,768]{2,1,0:T(8,128)}), f32[4,128,768]{2,1,0:T(8,128)S(1)}, u32[]{:S(2)}, u32[]{:S(2)}) async-start(f32[4,128,768]{2,1,0:T(8,128)} %all-reduce.5.cloned.1.call-done), calls=%async_computation.1 | async-start | bytes 3145728 | tf_op jit(solution)/shard_map/all_to_all | solution.py:48
  686.1 7.7 %copy-start.1 = (bf16[512,4096]{1,0:T(8,128)(2,1)S(1)}, bf16[512,4096]{1,0:T(8,128)(2,1)}, u32[]{:S(2)}) copy-start(bf16[512,4096]{1,0:T(8,128)(2,1)} %copy-done) | copy-start | bytes 12582916
Sparse Core Ops, SparseCore 0:
  45.6 563.5 all-reduce.6
  631.7 50.5 all-reduce.4
where the time goes:
time: 716 us
  waiting for transfers between devices  621 us (87%)
  matrix products  38 us (5%)
  blocking collectives  16 us (2%)
  other arithmetic  15.5 us (2%)
  between operations  14.2 us (2%)
  local copies, waits for them, and re-layouts  7.88 us (1%)
    psum x1, waiting for transfers between devices, local(): pre_gate, pre_up = lax.psum((part_gate, part_up), 'dp')  563 us
    psum x1, waiting for transfers between devices, local(): whole = lax.psum(back, 'section')  50.3 us
    all_to_all x1, blocking collectives, local(): lax.all_to_all(send_x, 'expert', split_axis=0, concat_axis=0, tiled=True)  16 us
  transfers between devices with their start and end apart: 3, of which 3 were waited for; matrix products, arithmetic and copies ran while one was open for 2% of the time, Pallas kernels for 0%

commit v1 on v0

v1 whole, which is shorter than its diff:
```python
import functools

import jax
import jax.numpy as jnp
from jax import lax
from jax.experimental import pallas as pl
from jax.experimental.pallas import tpu as pltpu
from jax.sharding import PartitionSpec as P

BF, HALF, F32 = jnp.bfloat16, jnp.float16, jnp.float32
SCALE = 16.0
OUT, MID, BACK = [(0, 1), (3, 2)], [(1, 2), (2, 1)], [(1, 0), (2, 3)]
MIB = 1024 * 1024


def dot(a, b, dims=((1,), (0,))):
    return lax.dot_general(a, b, (dims, ((), ())), preferred_element_type=F32)


def swap(value, axis, stride):
    n = lax.axis_size(axis)
    return lax.ppermute(value, axis, [(i, i ^ stride) for i in range(n)])


def gather_expert(value):
    n = lax.axis_size("expert")
    me = lax.axis_index("expert")
    held, stage, stride = value, 0, n // 2
    while stride >= 1:
        other = swap(held, "expert", stride)
        low = (me & stride) == 0
        held = jnp.stack([jnp.where(low, held, other), jnp.where(low, other, held)], axis=stage)
        stage, stride = stage + 1, stride // 2
    return held.reshape((n,) + value.shape)


def scatter_expert(value):
    n = lax.axis_size("expert")
    me = lax.axis_index("expert")
    stride = 1
    while stride < n:
        value = value.reshape((-1, 2) + value.shape[1:])
        low = (me & stride) == 0
        keep = jnp.where(low, value[:, 0], value[:, 1])
        send = jnp.where(low, value[:, 1], value[:, 0])
        got = swap(send, "expert", stride)
        value = (keep.astype(F32) + got.astype(F32)).astype(BF)
        stride *= 2
    return value[0]


def chunks_of(total):
    body, ramp = 512, [256, 256]
    while ramp and total < 2 * sum(ramp) + body:
        body = ramp.pop()
    count, rest = divmod(total - 2 * sum(ramp), body)
    assert rest == 0 and count > 0
    at = 0
    for size in ramp + [body] * count + ramp[::-1]:
        yield at, size
        at += size


ANY = pl.BlockSpec(memory_space=pl.ANY)
TOKEN = jax.ShapeDtypeStruct((8, 128), F32)


def whole(shape):
    return pl.BlockSpec(shape, lambda i: (0,) * len(shape))


class Part:
    def __init__(self, at, n):
        self.at, self.n, self.wide = at, n, min(n, 256)
        self.steps = n // self.wide

    def inside(self, height):
        first, steps = self.at // self.wide, self.steps
        return pl.BlockSpec((height, self.wide), lambda i: (0, first + jnp.minimum(i, steps - 1)))

    def own(self, height):
        steps = self.steps
        return pl.BlockSpec((height, 2 * self.wide), lambda i: (0, jnp.minimum(i, steps - 1)))


def call(body, steps, ins, in_specs, outs, out_specs, alias, vmem):
    return pl.pallas_call(
        body,
        grid=(steps,),
        in_specs=in_specs,
        out_specs=out_specs,
        out_shape=outs,
        input_output_aliases=alias,
        compiler_params=pltpu.CompilerParams(vmem_limit_bytes=vmem),
        cost_estimate=pl.CostEstimate(flops=1, bytes_accessed=1, transcendentals=0),
    )(*ins)


def produce_body(x_ref, wg_ref, wu_ref, p_ref):
    n = wg_ref.shape[1]
    p_ref[:, :n] = dot(x_ref[...], wg_ref[...])
    p_ref[:, n:] = dot(x_ref[...], wu_ref[...])


def finish_body(first, x_ref, wg_ref, wu_ref, t_ref, pick_ref, cot_ref, back_in, acted_ref, gg_ref, ug_ref, back_ref):
    n = wg_ref.shape[1]

    @pl.when(first)
    def _():
        back_ref[...] = back_in[...]

    pre_gate, pre_up = t_ref[:, :n], t_ref[:, n:]
    sig = jax.nn.sigmoid(pre_gate)
    silu_v = pre_gate * sig
    cf = dot(pick_ref[...], cot_ref[...])
    gp = (cf * pre_up * sig * (1.0 + pre_gate * (1.0 - sig))).astype(BF)
    up = (cf * silu_v).astype(BF)
    acted = (silu_v * pre_up).astype(BF)
    acted_ref[...] = dot(pick_ref[...], acted, ((0,), (0,))).astype(BF)
    gg_ref[...] = dot(x_ref[...], gp, ((0,), (0,))).astype(BF)
    ug_ref[...] = dot(x_ref[...], up, ((0,), (0,))).astype(BF)
    back_ref[...] += dot(gp, wg_ref[...], ((1,), (1,))) + dot(up, wu_ref[...], ((1,), (1,)))


def main_call(token, x, wg, wu, make=None, end=None):
    rows, width = x.shape
    ins, in_specs = [token, x], [ANY, whole(x.shape)]
    outs, out_specs, alias = [TOKEN], [whole((8, 128))], {}
    end_steps = make_steps = 0
    if end is not None:
        part, t, pick, cot, acted, gg, ug, back = end
        end_steps = part.steps
        for arr, spec, into in (
            (wg, part.inside(width), None),
            (wu, part.inside(width), None),
            (t, part.own(rows), None),
            (pick, whole(pick.shape), None),
            (cot, part.inside(cot.shape[0]), None),
            (back, whole(back.shape), 4),
            (acted, ANY, 1),
            (gg, ANY, 2),
            (ug, ANY, 3),
        ):
            if arr is None:
                continue
            if into is not None:
                alias[len(ins)] = into
            ins.append(arr)
            in_specs.append(spec)
        outs += [jax.ShapeDtypeStruct(v, BF) for v in (cot.shape, wg.shape, wg.shape)]
        outs += [jax.ShapeDtypeStruct(back.shape, F32)]
        out_specs += [part.inside(cot.shape[0]), part.inside(width), part.inside(width), whole(back.shape)]
    if make is not None:
        make_steps, n = make.steps, make.n
        ins += [wg, wu]
        in_specs += [make.inside(width)] * 2
        outs.append(jax.ShapeDtypeStruct((rows, 2 * n), F32))
        out_specs.append(make.own(rows))
    n_in = len(ins)

    def body(*refs):
        i, o = refs[:n_in], refs[n_in:]
        step = pl.program_id(0)
        o[0][...] = jnp.zeros((8, 128), F32)
        if make is not None:

            @pl.when(step < make_steps)
            def _():
                produce_body(i[1], i[-2], i[-1], o[-1])

        if end is not None:

            @pl.when(step < end_steps)
            def _():
                finish_body(step == 0, *i[1:8], *o[1:5])

    return call(body, max(end_steps, make_steps), ins, in_specs, outs, out_specs, alias, 30 * MIB)


def pipeline(rows, cap, tokens, hit, rank, wg, wu, cot):
    groups, per = hit.shape
    width, hidden = wg.shape
    count = jnp.sum(hit.astype(F32), axis=1)
    first = jnp.cumsum(count) - count
    place = jnp.where(hit, first[:, None] + rank, -1.0).reshape(1, groups * per)
    row = jnp.arange(rows, dtype=F32)[:, None]
    take = (row == place).astype(BF)
    slot = jnp.arange(cap, dtype=F32)[None, :]
    slot_row = jnp.where(slot < count[:, None], first[:, None] + slot, -1.0).reshape(1, groups * cap)
    pick = (row == slot_row).astype(BF)
    x = dot(take, tokens).astype(BF)

    dp = lax.axis_index("dp")
    inner = (dp == 1) | (dp == 2)
    parts = [Part(at, n) for at, n in chunks_of(hidden)]
    acted = gg = ug = None
    back = jnp.zeros((rows, width), F32)
    token = jnp.zeros((8, 128), F32)
    p, a, q, b, t, c = {}, {}, {}, {}, {}, {}
    last = len(parts)

    def main(make, end):
        nonlocal token, acted, gg, ug, back
        done = end >= 0
        args = None
        if done:
            both = jnp.where(inner, t.pop(end), c.pop(end)).astype(F32) * (1.0 / SCALE)
            args = (parts[end], both, pick, cot, acted, gg, ug, back)
        out = main_call(token, x, wg, wu, parts[make] if make < last else None, args)
        token = out[0]
        if done:
            acted, gg, ug, back = out[1:5]
        if make < last:
            p[make] = out[-1] * SCALE
            a[make] = lax.ppermute(p[make].astype(HALF), "dp", OUT)

    main(0, -1)
    main(1, -1)
    for k in range(last + 2):
        if k < last:
            q[k] = (p.pop(k) + a.pop(k).astype(F32) + token[0, 0]).astype(HALF)
            b[k] = lax.ppermute(q[k], "dp", MID)
        if 1 <= k <= last:
            t[k - 1] = (q.pop(k - 1).astype(F32) + b.pop(k - 1).astype(F32) + token[0, 0]).astype(HALF)
            c[k - 1] = lax.ppermute(t[k - 1], "dp", BACK)
        after = [v[:8, :128].astype(F32) for v in (q.get(k), t.get(k - 1)) if v is not None]
        if after:
            token = sum(after)
        if k >= 2 or k + 2 < last:
            main(k + 2, k - 2)
    own = dot(take, back.astype(BF), ((0,), (0,))).astype(BF)
    return acted, gg, ug, own


def local(tokens, expert_ids, w_gate, w_up, cotangent):
    rows, width = tokens.shape
    experts = lax.axis_size("expert")
    cap = min(rows, 4 * rows // experts)
    wg, wu, cot = w_gate[0], w_up[0], cotangent[0]
    me = lax.axis_index("expert")
    ids = jnp.pad(expert_ids.astype(BF), ((0, 0), (0, 126)))
    held = gather_expert(jnp.concatenate([tokens, ids], axis=1))
    all_tokens, all_ids = held[:, :, :width], held[:, :, width : width + 2]
    hit = jnp.any(all_ids == me.astype(BF), axis=2)
    before = (jnp.arange(rows)[:, None] < jnp.arange(rows)[None, :]).astype(BF)
    rank = dot(hit.astype(BF), before)
    slots = experts * cap
    sizes = sorted({slots * part // 16 for part in (4, 6, 8, 12, 16)})
    filled = jnp.sum(hit.astype(jnp.int32))
    which = jnp.sum((filled > jnp.array(sizes[:-1], jnp.int32)).astype(jnp.int32))
    acted, gg, ug, own = lax.switch(
        which,
        [functools.partial(pipeline, size, cap) for size in sizes],
        all_tokens.reshape(experts * rows, width),
        hit,
        rank,
        wg,
        wu,
        cot,
    )
    part = scatter_expert(own.reshape(experts, rows, width))
    if lax.axis_size("section") == 2:
        total = part.astype(F32) + swap(part, "section", 1).astype(F32)
    else:
        total = lax.psum(part.astype(F32), "section")
    return acted[None], total.astype(BF), gg[None], ug[None]


def solution(mesh):
    placed = (
        P("expert", "dp"),
        P("expert", None),
        P("expert", "dp", "section"),
        P("expert", "dp", "section"),
        P("expert", None, "section"),
    )
    return jax.shard_map(
        local,
        mesh=mesh,
        in_specs=placed,
        out_specs=(
            P("expert", None, "section"),
            P("expert", "dp"),
            P("expert", "dp", "section"),
            P("expert", "dp", "section"),
        ),
        check_vma=False,
    )
```

time: 716 us -> 280 us (0.39)
  waiting for transfers between devices: 621 us -> 27.3 us
  starting transfers between devices: 4.04 us -> 152 us
  matrix products: 38 us -> 1.71 us
  Pallas kernels: 0 us -> 35.9 us
  loops' own time: 0 us -> 27.5 us
  blocking collectives: 16 us -> 0 us
  between operations: 14.2 us -> 1.57 us
    psum x2 -> x0, waiting for transfers between devices: 614 us -> none  [the longest x1 563 us: local(): pre_gate, pre_up = lax.psum((part_gate, part_up), 'dp')]
    ppermute x0 -> x35, starting transfers between devices: none -> 152 us  [the longest x5 81.6 us: swap(): return lax.ppermute(value, axis, [(i, i ^ stride) for i in range(n)])]
    dot_general x6 -> x3, matrix products: 38 us -> 1.71 us  [dot(): return lax.dot_general(a, b, (dims, ((), ())), preferred_element_type=F32)]
    pallas_call x0 -> x14, Pallas kernels: none -> 35.9 us  [call(): pl.pallas_call(body, grid=(steps,), in_specs=in_specs, out_specs=out_spec...]
    another operation x0 -> x1, loops' own time: none -> 27.5 us  [local(): lax.switch(which, [functools.partial(pipeline, size, cap) for size in siz...]
    ppermute x0 -> x35, waiting for transfers between devices: none -> 27.3 us  [the longest x5 18.9 us: swap(): return lax.ppermute(value, axis, [(i, i ^ stride) for i in range(n)])]
    all_to_all x1 -> x0, blocking collectives: 16 us -> none  [local(): lax.all_to_all(send_x, 'expert', split_axis=0, concat_axis=0, tiled=True)]
    slice x2 -> x13, local copies, waits for them, and re-layouts: 0.18 us -> 7.77 us  [the longest x10 5.13 us: pipeline(): q[k] = (p.pop(k) + a.pop(k).astype(F32) + token[0, 0]).astype(HALF)]
  transfers between devices with their start and end apart: 3 -> 35, of which waited for: 3 -> 8; matrix products, arithmetic and copies ran while one was open for 2% -> 8% of each run, Pallas kernels for 0% -> 12%
where the time goes in v1:
time: 280 us; the launch traced here: 279 us
  starting transfers between devices  152 us (54%)
  Pallas kernels  35.9 us (13%)
  loops' own time  27.5 us (10%)
  waiting for transfers between devices  27.3 us (10%)
  other arithmetic  22.1 us (8%)
  local copies, waits for them, and re-layouts  10.1 us (4%)
    ppermute x5, starting transfers between devices, swap(): return lax.ppermute(value, axis, [(i, i ^ stride) for i in range(n)])  81.6 us
    ppermute x10, starting transfers between devices, main(): a[make] = lax.ppermute(p[make].astype(HALF), 'dp', OUT)  50.4 us
    pallas_call x14, Pallas kernels, call(): pl.pallas_call(body, grid=(steps,), in_specs=in_specs, out_specs=out_spec...  35.9 us
    another operation x1, loops' own time, local(): lax.switch(which, [functools.partial(pipeline, size, cap) for size in siz...  27.5 us
    ppermute x5, waiting for transfers between devices, swap(): return lax.ppermute(value, axis, [(i, i ^ stride) for i in range(n)])  18.9 us
    ppermute x10, starting transfers between devices, pipeline(): c[k - 1] = lax.ppermute(t[k - 1], 'dp', BACK)  13.5 us
    ppermute x10, waiting for transfers between devices, pipeline(): c[k - 1] = lax.ppermute(t[k - 1], 'dp', BACK)  8.4 us
    convert_element_type x10, other arithmetic, pipeline(): q[k] = (p.pop(k) + a.pop(k).astype(F32) + token[0, 0]).astype(HALF)  7.37 us
  transfers between devices with their start and end apart: 35, of which 8 were waited for; matrix products, arithmetic and copies ran while one was open for 8% of the time, Pallas kernels for 12%

profile of v1, /device:TPU:0, one launch (start us, length us, event | category | flops | bytes accessed | tf_op | source)
XLA Modules:
  0.0 278.6 jit_solution(17934578716452633980)
XLA Ops:
  2.4 3.0 %collective-permute-start.150 = (bf16[128,896]{1,0:T(8,128)(2,1)S(1)}, bf16[128,896]{1,0:T(8,128)(2,1)S(1)}, u32[]{:S(2)}, u32[]{:S(2)}) collective-permute-start(bf16[128,896]{1,0:T(8,128)(2,1)S(1)} %fusion.23), channel_id=1, source_target_pairs={{0,8},{4,12},{8,0},{12,4},{1,9},{5,13},{9,1},{13,5},{2,10},{6,14},... | collective-permute-start | bytes 688136 | tf_op jit(solution)/shard_map/ppermute | solution.py:22
  5.4 5.6 %collective-permute-done.150 = bf16[128,896]{1,0:T(8,128)(2,1)S(1)} collective-permute-done((bf16[128,896]{1,0:T(8,128)(2,1)S(1)}, bf16[128,896]{1,0:T(8,128)(2,1)S(1)}, u32[]{:S(2)}, u32[]{:S(2)}) %collective-permute-start.150) | collective-permute-done | bytes 229408 | tf_op jit(solution)/shard_map/ppermute | solution.py:22
  17.2 170.2 %conditional.1 = (bf16[512,4096]{1,0:T(8,128)(2,1)}, bf16[768,4096]{1,0:T(8,128)(2,1)}, bf16[768,4096]{1,0:T(8,128)(2,1)}, bf16[2,2,128,768]{3,2,1,0:T(8,128)(2,...) conditional(s32[]{:T(128)} %clamp.3, ...), branch_computations={%region_3.6_spmd, %region_6.9_spmd, %region_9.12_spmd, %region_12.... | conditional | flops 870482432 | bytes 327539232 | solution.py:251
  19.5 4.0 %collective-permute-start.1 = (f16[128,512]{1,0:T(8,128)(2,1)S(1)}, f16[128,512]{1,0:T(8,128)(2,1)S(1)}, u32[]{:S(2)}, u32[]{:S(2)}) collective-permute-start(f16[128,512]{1,0:T(8,128)(2,1)S(1)} %multiply_convert_fusion.8), channel_id=1, source_target_pairs={{0,1},{3,2},{4,5},{7,6},{8,9},{11,10},{12,13},{15,14},{16,17},{19,... | collective-permute-start | bytes 393224 | tf_op jit(solution)/shard_map/cond/branch_0_fun/ppermute | solution.py:215
  23.9 3.0 %collective-permute-start = (f16[128,512]{1,0:T(8,128)(2,1)S(1)}, f16[128,512]{1,0:T(8,128)(2,1)S(1)}, u32[]{:S(2)}, u32[]{:S(2)}) collective-permute-start(f16[128,512]{1,0:T(8,128)(2,1)S(1)} %multiply_convert_fusion.9), channel_id=1, source_target_pairs={{0,1},{3,2},{4,5},{7,6},{8,9},{11,10},{12,13},{15,14},{16,17},{19,... | collective-permute-start | bytes 393224 | tf_op jit(solution)/shard_map/cond/branch_0_fun/ppermute | solution.py:215
  33.2 7.2 %collective-permute-start.4 = (f16[128,1024]{1,0:T(8,128)(2,1)S(1)}, f16[128,1024]{1,0:T(8,128)(2,1)S(1)}, u32[]{:S(2)}, u32[]{:S(2)}) collective-permute-start(f16[128,1024]{1,0:T(8,128)(2,1)S(1)} %multiply_convert_fusion.4), channel_id=1, source_target_pairs={{0,1},{3,2},{4,5},{7,6},{8,9},{11,10},{12,13},{15,14},{16,17},{19,... | collective-permute-start | bytes 786440 | tf_op jit(solution)/shard_map/cond/branch_0_fun/ppermute | solution.py:215
  44.7 4.4 %collective-permute-start.3 = (f16[128,1024]{1,0:T(8,128)(2,1)S(1)}, f16[128,1024]{1,0:T(8,128)(2,1)S(1)}, u32[]{:S(2)}, u32[]{:S(2)}) collective-permute-start(f16[128,1024]{1,0:T(8,128)(2,1)S(1)} %multiply_convert_fusion.5), channel_id=1, source_target_pairs={{0,1},{3,2},{4,5},{7,6},{8,9},{11,10},{12,13},{15,14},{16,17},{19,... | collective-permute-start | bytes 786440 | tf_op jit(solution)/shard_map/cond/branch_0_fun/ppermute | solution.py:215
  56.2 7.5 %collective-permute-start.10 = (f16[128,1024]{1,0:T(8,128)(2,1)S(1)}, f16[128,1024]{1,0:T(8,128)(2,1)S(1)}, u32[]{:S(2)}, u32[]{:S(2)}) collective-permute-start(f16[128,1024]{1,0:T(8,128)(2,1)S(1)} %multiply_convert_fusion.2), channel_id=1, source_target_pairs={{0,1},{3,2},{4,5},{7,6},{8,9},{11,10},{12,13},{15,14},{16,17},{19,... | collective-permute-start | bytes 786440 | tf_op jit(solution)/shard_map/cond/branch_0_fun/ppermute | solution.py:215
  72.8 6.1 %collective-permute-start.9 = (f16[128,1024]{1,0:T(8,128)(2,1)S(1)}, f16[128,1024]{1,0:T(8,128)(2,1)S(1)}, u32[]{:S(2)}, u32[]{:S(2)}) collective-permute-start(f16[128,1024]{1,0:T(8,128)(2,1)S(1)} %multiply_convert_fusion.3), channel_id=1, source_target_pairs={{0,1},{3,2},{4,5},{7,6},{8,9},{11,10},{12,13},{15,14},{16,17},{19,... | collective-permute-start | bytes 786440 | tf_op jit(solution)/shard_map/cond/branch_0_fun/ppermute | solution.py:215
  81.1 4.0 %branch_0_fun.20 = (f32[8,128]{1,0:T(8,128)S(1)}, bf16[512,4096]{1,0:T(8,128)(2,1)}, bf16[768,4096]{1,0:T(8,128)(2,1)}, bf16[768,4096]{1,0:T(8,128)(2,1)}, f32[1...) custom-call(f32[8,128]{1,0:T(8,128)S(1)} %convert_add_fusion.5.refs_, ...), custom_call_target="tpu_custom_call", output_to_operand_aliasing={{4}: (7, {}), {1}: (8, {}), {2}: (9, {}), {3}: (10, {})} | custom-call | flops 1 | bytes 1 | tf_op jit(solution)/shard_map/cond/branch_0_fun/pallas_call | solution.py:87
  85.1 4.6 %collective-permute-start.16 = (f16[128,1024]{1,0:T(8,128)(2,1)S(1)}, f16[128,1024]{1,0:T(8,128)(2,1)S(1)}, u32[]{:S(2)}, u32[]{:S(2)}) collective-permute-start(f16[128,1024]{1,0:T(8,128)(2,1)S(1)} %multiply_convert_fusion), channel_id=1, source_target_pairs={{0,1},{3,2},{4,5},{7,6},{8,9},{11,10},{12,13},{15,14},{16,17},{19,... | collective-permute-start | bytes 786440 | tf_op jit(solution)/shard_map/cond/branch_0_fun/ppermute | solution.py:215
  93.8 4.0 %branch_0_fun.21 = (f32[8,128]{1,0:T(8,128)S(1)}, bf16[512,4096]{1,0:T(8,128)(2,1)}, bf16[768,4096]{1,0:T(8,128)(2,1)}, bf16[768,4096]{1,0:T(8,128)(2,1)}, f32[1...) custom-call(f32[8,128]{1,0:T(8,128)S(1)} %convert_add_fusion.4.refs_, ...), custom_call_target="tpu_custom_call", output_to_operand_aliasing={{4}: (7, {}), {1}: (8, {}), {2}: (9, {}), {3}: (10, {})} | custom-call | flops 1 | bytes 1 | tf_op jit(solution)/shard_map/cond/branch_0_fun/pallas_call | solution.py:87
  98.4 4.5 %collective-permute-start.15 = (f16[128,1024]{1,0:T(8,128)(2,1)S(1)}, f16[128,1024]{1,0:T(8,128)(2,1)S(1)}, u32[]{:S(2)}, u32[]{:S(2)}) collective-permute-start(f16[128,1024]{1,0:T(8,128)(2,1)S(1)} %multiply_convert_fusion.1), channel_id=1, source_target_pairs={{0,1},{3,2},{4,5},{7,6},{8,9},{11,10},{12,13},{15,14},{16,17},{19,... | collective-permute-start | bytes 786440 | tf_op jit(solution)/shard_map/cond/branch_0_fun/ppermute | solution.py:215
  106.9 3.5 %branch_0_fun.22 = (f32[8,128]{1,0:T(8,128)S(1)}, bf16[512,4096]{1,0:T(8,128)(2,1)}, bf16[768,4096]{1,0:T(8,128)(2,1)}, bf16[768,4096]{1,0:T(8,128)(2,1)}, f32[1...) custom-call(f32[8,128]{1,0:T(8,128)S(1)} %convert_add_fusion.3.refs_, ...), custom_call_target="tpu_custom_call", output_to_operand_aliasing={{4}: (7, {}), {1}: (8, {}), {2}: (9, {}), {3}: (10, {})} | custom-call | flops 1 | bytes 1 | tf_op jit(solution)/shard_map/cond/branch_0_fun/pallas_call | solution.py:87
  110.9 4.6 %collective-permute-start.22 = (f16[128,512]{1,0:T(8,128)(2,1)S(1)}, f16[128,512]{1,0:T(8,128)(2,1)S(1)}, u32[]{:S(2)}, u32[]{:S(2)}) collective-permute-start(f16[128,512]{1,0:T(8,128)(2,1)S(1)} %multiply_convert_fusion.6), channel_id=1, source_target_pairs={{0,1},{3,2},{4,5},{7,6},{8,9},{11,10},{12,13},{15,14},{16,17},{19,... | collective-permute-start | bytes 393224 | tf_op jit(solution)/shard_map/cond/branch_0_fun/ppermute | solution.py:215
  119.1 3.5 %branch_0_fun.23 = (f32[8,128]{1,0:T(8,128)S(1)}, bf16[512,4096]{1,0:T(8,128)(2,1)}, bf16[768,4096]{1,0:T(8,128)(2,1)}, bf16[768,4096]{1,0:T(8,128)(2,1)}, f32[1...) custom-call(f32[8,128]{1,0:T(8,128)S(1)} %convert_add_fusion.2.refs_, ...), custom_call_target="tpu_custom_call", output_to_operand_aliasing={{4}: (7, {}), {1}: (8, {}), {2}: (9, {}), {3}: (10, {})} | custom-call | flops 1 | bytes 1 | tf_op jit(solution)/shard_map/cond/branch_0_fun/pallas_call | solution.py:87
  122.6 4.6 %collective-permute-start.21 = (f16[128,512]{1,0:T(8,128)(2,1)S(1)}, f16[128,512]{1,0:T(8,128)(2,1)S(1)}, u32[]{:S(2)}, u32[]{:S(2)}) collective-permute-start(f16[128,512]{1,0:T(8,128)(2,1)S(1)} %multiply_convert_fusion.7), channel_id=1, source_target_pairs={{0,1},{3,2},{4,5},{7,6},{8,9},{11,10},{12,13},{15,14},{16,17},{19,... | collective-permute-start | bytes 393224 | tf_op jit(solution)/shard_map/cond/branch_0_fun/ppermute | solution.py:215
  131.2 3.1 %branch_0_fun.24 = (f32[8,128]{1,0:T(8,128)S(1)}, bf16[512,4096]{1,0:T(8,128)(2,1)}, bf16[768,4096]{1,0:T(8,128)(2,1)}, bf16[768,4096]{1,0:T(8,128)(2,1)}, f32[128,768]{1,0:T(8,128)S(1)}) custom-call(f32[8,128]{1,0:T(8,128)S(1)} %convert_add_fusion.1.refs_0_, ...), custom_call_target="tpu_custom_call", output_to_operand_aliasing={{4}: (7, {}), {1}: (8, {}), {2}: (9, {}), {3}: (10, {})} | custom-call | flops 1 | bytes 1 | tf_op jit(solution)/shard_map/cond/branch_0_fun/pallas_call | solution.py:87
  140.9 3.1 %branch_0_fun.25 = (f32[8,128]{1,0:T(8,128)S(1)}, bf16[512,4096]{1,0:T(8,128)(2,1)}, bf16[768,4096]{1,0:T(8,128)(2,1)}, bf16[768,4096]{1,0:T(8,128)(2,1)}, f32[128,768]{1,0:T(8,128)S(1)}) custom-call(f32[8,128]{1,0:T(8,128)S(1)} %convert_add_fusion.refs_0_, ...), custom_call_target="tpu_custom_call", output_to_operand_aliasing={{4}: (7, {}), {1}: (8, {}), {2}: (9, {}), {3}: (10, {})} | custom-call | flops 1 | bytes 1 | tf_op jit(solution)/shard_map/cond/branch_0_fun/pallas_call | solution.py:87
  149.0 4.9 %collective-permute-done.29 = f16[128,512]{1,0:T(8,128)(2,1)S(1)} collective-permute-done((f16[128,512]{1,0:T(8,128)(2,1)S(1)}, f16[128,512]{1,0:T(8,128)(2,1)S(1)}, u32[]{:S(2)}, u32[]{:S(2)}) %collective-permute-start.29) | collective-permute-done | bytes 131104 | tf_op jit(solution)/shard_map/cond/branch_0_fun/ppermute | solution.py:225
  187.4 28.3 %collective-permute-start.152 = (bf16[2,128,768]{2,1,0:T(8,128)(2,1)S(1)}, bf16[2,128,768]{2,1,0:T(8,128)(2,1)S(1)}, u32[]{:S(2)}, u32[]{:S(2)}) collective-permute-start(bf16[2,128,768]{2,1,0:T(8,128)(2,1)S(1)} %broadcast_select_fusion), channel_id=1, source_target_pairs={{0,4},{4,0},{8,12},{12,8},{1,5},{5,1},{9,13},{13,9},{2,6},{6,2},{1... | collective-permute-start | bytes 1179656 | tf_op jit(solution)/shard_map/ppermute | solution.py:22
  217.2 48.7 %collective-permute-start.153 = (bf16[1,128,768]{2,1,0:T(8,128)(2,1)S(1)}, bf16[1,128,768]{2,1,0:T(8,128)(2,1)S(1)}, u32[]{:S(2)}, u32[]{:S(2)}) collective-permute-start(bf16[1,128,768]{2,1,0:T(8,128)(2,1)S(1)} %select_bitcast_fusion.14), channel_id=1, source_target_pairs={{0,8},{4,12},{8,0},{12,4},{1,9},{5,13},{9,1},{13,5},{2,10},{6,14},... | collective-permute-start | bytes 589832 | tf_op jit(solution)/shard_map/ppermute | solution.py:22
  265.9 5.2 %collective-permute-done.153 = bf16[1,128,768]{2,1,0:T(8,128)(2,1)S(1)} collective-permute-done((bf16[1,128,768]{2,1,0:T(8,128)(2,1)S(1)}, bf16[1,128,768]{2,1,0:T(8,128)(2,1)S(1)}, u32[]{:S(2)}, u32[]{:S(2)}) %collective-permute-start.153) | collective-permute-done | bytes 196640 | tf_op jit(solution)/shard_map/ppermute | solution.py:22
  272.7 4.9 %collective-permute-done.154 = bf16[128,768]{1,0:T(8,128)(2,1)S(1)} collective-permute-done((bf16[128,768]{1,0:T(8,128)(2,1)S(1)}, bf16[128,768]{1,0:T(8,128)(2,1)S(1)}, u32[]{:S(2)}, u32[]{:S(2)}) %collective-permute-start.154) | collective-permute-done | bytes 196640 | tf_op jit(solution)/shard_map/ppermute | solution.py:22
  (174 shorter events, 77.4 us)
Async XLA Ops:
  28.2 12.1 %collective-permute-start.2 = (f16[128,512]{1,0:T(8,128)(2,1)S(1)}, f16[128,512]{1,0:T(8,128)(2,1)S(1)}, u32[]{:S(2)}, u32[]{:S(2)}) collective-permute-start(f16[128,512]{1,0:T(8,128)(2,1)S(1)} %add_convert_fusion.19), channel_id=1, source_target_pairs={{1,2},{2,1},{5,6},{6,5},{9,10},{10,9},{13,14},{14,13},{17,18},{18,... | collective-permute-start | bytes 393224 | tf_op jit(solution)/shard_map/cond/branch_0_fun/ppermute | solution.py:222
  32.4 17.3 %collective-permute-start.5 = (f16[128,512]{1,0:T(8,128)(2,1)S(1)}, f16[128,512]{1,0:T(8,128)(2,1)S(1)}, u32[]{:S(2)}, u32[]{:S(2)}) collective-permute-start(f16[128,512]{1,0:T(8,128)(2,1)S(1)} %add_convert_fusion.18), channel_id=1, source_target_pairs={{1,2},{2,1},{5,6},{6,5},{9,10},{10,9},{13,14},{14,13},{17,18},{18,... | collective-permute-start | bytes 393224 | tf_op jit(solution)/shard_map/cond/branch_0_fun/ppermute | solution.py:222
  33.2 18.5 %collective-permute-start.4 = (f16[128,1024]{1,0:T(8,128)(2,1)S(1)}, f16[128,1024]{1,0:T(8,128)(2,1)S(1)}, u32[]{:S(2)}, u32[]{:S(2)}) collective-permute-start(f16[128,1024]{1,0:T(8,128)(2,1)S(1)} %multiply_convert_fusion.4), channel_id=1, source_target_pairs={{0,1},{3,2},{4,5},{7,6},{8,9},{11,10},{12,13},{15,14},{16,17},{19,... | collective-permute-start | bytes 786440 | tf_op jit(solution)/shard_map/cond/branch_0_fun/ppermute | solution.py:215
  44.7 19.6 %collective-permute-start.3 = (f16[128,1024]{1,0:T(8,128)(2,1)S(1)}, f16[128,1024]{1,0:T(8,128)(2,1)S(1)}, u32[]{:S(2)}, u32[]{:S(2)}) collective-permute-start(f16[128,1024]{1,0:T(8,128)(2,1)S(1)} %multiply_convert_fusion.5), channel_id=1, source_target_pairs={{0,1},{3,2},{4,5},{7,6},{8,9},{11,10},{12,13},{15,14},{16,17},{19,... | collective-permute-start | bytes 786440 | tf_op jit(solution)/shard_map/cond/branch_0_fun/ppermute | solution.py:215
  50.4 13.4 %collective-permute-start.8 = (f16[128,512]{1,0:T(8,128)(2,1)S(1)}, f16[128,512]{1,0:T(8,128)(2,1)S(1)}, u32[]{:S(2)}, u32[]{:S(2)}) collective-permute-start(f16[128,512]{1,0:T(8,128)(2,1)S(1)} %add_convert_fusion.16), channel_id=1, source_target_pairs={{1,0},{2,3},{5,4},{6,7},{9,8},{10,11},{13,12},{14,15},{17,16},{18,... | collective-permute-start | bytes 393224 | tf_op jit(solution)/shard_map/cond/branch_0_fun/ppermute | solution.py:225
  52.5 13.3 %collective-permute-start.7 = (f16[128,1024]{1,0:T(8,128)(2,1)S(1)}, f16[128,1024]{1,0:T(8,128)(2,1)S(1)}, u32[]{:S(2)}, u32[]{:S(2)}) collective-permute-start(f16[128,1024]{1,0:T(8,128)(2,1)S(1)} %add_convert_fusion.11), channel_id=1, source_target_pairs={{1,2},{2,1},{5,6},{6,5},{9,10},{10,9},{13,14},{14,13},{17,18},{18,... | collective-permute-start | bytes 786440 | tf_op jit(solution)/shard_map/cond/branch_0_fun/ppermute | solution.py:222
  56.2 15.0 %collective-permute-start.10 = (f16[128,1024]{1,0:T(8,128)(2,1)S(1)}, f16[128,1024]{1,0:T(8,128)(2,1)S(1)}, u32[]{:S(2)}, u32[]{:S(2)}) collective-permute-start(f16[128,1024]{1,0:T(8,128)(2,1)S(1)} %multiply_convert_fusion.2), channel_id=1, source_target_pairs={{0,1},{3,2},{4,5},{7,6},{8,9},{11,10},{12,13},{15,14},{16,17},{19,... | collective-permute-start | bytes 786440 | tf_op jit(solution)/shard_map/cond/branch_0_fun/ppermute | solution.py:215
  65.1 13.8 %collective-permute-start.11 = (f16[128,1024]{1,0:T(8,128)(2,1)S(1)}, f16[128,1024]{1,0:T(8,128)(2,1)S(1)}, u32[]{:S(2)}, u32[]{:S(2)}) collective-permute-start(f16[128,1024]{1,0:T(8,128)(2,1)S(1)} %add_convert_fusion.10), channel_id=1, source_target_pairs={{1,2},{2,1},{5,6},{6,5},{9,10},{10,9},{13,14},{14,13},{17,18},{18,... | collective-permute-start | bytes 786440 | tf_op jit(solution)/shard_map/cond/branch_0_fun/ppermute | solution.py:222
  66.5 14.4 %collective-permute-start.12 = (f16[128,1024]{1,0:T(8,128)(2,1)S(1)}, f16[128,1024]{1,0:T(8,128)(2,1)S(1)}, u32[]{:S(2)}, u32[]{:S(2)}) collective-permute-start(f16[128,1024]{1,0:T(8,128)(2,1)S(1)} %add_convert_fusion.9), channel_id=1, source_target_pairs={{1,0},{2,3},{5,4},{6,7},{9,8},{10,11},{13,12},{14,15},{17,16},{18,... | collective-permute-start | bytes 786440 | tf_op jit(solution)/shard_map/cond/branch_0_fun/ppermute | solution.py:225
  72.0 19.6 %collective-permute-start.13 = (f16[128,1024]{1,0:T(8,128)(2,1)S(1)}, f16[128,1024]{1,0:T(8,128)(2,1)S(1)}, u32[]{:S(2)}, u32[]{:S(2)}) collective-permute-start(f16[128,1024]{1,0:T(8,128)(2,1)S(1)} %add_convert_fusion.8), channel_id=1, source_target_pairs={{1,2},{2,1},{5,6},{6,5},{9,10},{10,9},{13,14},{14,13},{17,18},{18,... | collective-permute-start | bytes 786440 | tf_op jit(solution)/shard_map/cond/branch_0_fun/ppermute | solution.py:222
  72.8 17.4 %collective-permute-start.9 = (f16[128,1024]{1,0:T(8,128)(2,1)S(1)}, f16[128,1024]{1,0:T(8,128)(2,1)S(1)}, u32[]{:S(2)}, u32[]{:S(2)}) collective-permute-start(f16[128,1024]{1,0:T(8,128)(2,1)S(1)} %multiply_convert_fusion.3), channel_id=1, source_target_pairs={{0,1},{3,2},{4,5},{7,6},{8,9},{11,10},{12,13},{15,14},{16,17},{19,... | collective-permute-start | bytes 786440 | tf_op jit(solution)/shard_map/cond/branch_0_fun/ppermute | solution.py:215
  79.6 14.1 %collective-permute-start.14 = (f16[128,1024]{1,0:T(8,128)(2,1)S(1)}, f16[128,1024]{1,0:T(8,128)(2,1)S(1)}, u32[]{:S(2)}, u32[]{:S(2)}) collective-permute-start(f16[128,1024]{1,0:T(8,128)(2,1)S(1)} %add_convert_fusion.7), channel_id=1, source_target_pairs={{1,0},{2,3},{5,4},{6,7},{9,8},{10,11},{13,12},{14,15},{17,16},{18,... | collective-permute-start | bytes 786440 | tf_op jit(solution)/shard_map/cond/branch_0_fun/ppermute | solution.py:225
  85.1 17.8 %collective-permute-start.16 = (f16[128,1024]{1,0:T(8,128)(2,1)S(1)}, f16[128,1024]{1,0:T(8,128)(2,1)S(1)}, u32[]{:S(2)}, u32[]{:S(2)}) collective-permute-start(f16[128,1024]{1,0:T(8,128)(2,1)S(1)} %multiply_convert_fusion), channel_id=1, source_target_pairs={{0,1},{3,2},{4,5},{7,6},{8,9},{11,10},{12,13},{15,14},{16,17},{19,... | collective-permute-start | bytes 786440 | tf_op jit(solution)/shard_map/cond/branch_0_fun/ppermute | solution.py:215
  90.9 13.4 %collective-permute-start.17 = (f16[128,1024]{1,0:T(8,128)(2,1)S(1)}, f16[128,1024]{1,0:T(8,128)(2,1)S(1)}, u32[]{:S(2)}, u32[]{:S(2)}) collective-permute-start(f16[128,1024]{1,0:T(8,128)(2,1)S(1)} %add_convert_fusion.6), channel_id=1, source_target_pairs={{1,2},{2,1},{5,6},{6,5},{9,10},{10,9},{13,14},{14,13},{17,18},{18,... | collective-permute-start | bytes 786440 | tf_op jit(solution)/shard_map/cond/branch_0_fun/ppermute | solution.py:222
  92.4 14.4 %collective-permute-start.18 = (f16[128,1024]{1,0:T(8,128)(2,1)S(1)}, f16[128,1024]{1,0:T(8,128)(2,1)S(1)}, u32[]{:S(2)}, u32[]{:S(2)}) collective-permute-start(f16[128,1024]{1,0:T(8,128)(2,1)S(1)} %add_convert_fusion.5), channel_id=1, source_target_pairs={{1,0},{2,3},{5,4},{6,7},{9,8},{10,11},{13,12},{14,15},{17,16},{18,... | collective-permute-start | bytes 786440 | tf_op jit(solution)/shard_map/cond/branch_0_fun/ppermute | solution.py:225
  98.4 17.1 %collective-permute-start.15 = (f16[128,1024]{1,0:T(8,128)(2,1)S(1)}, f16[128,1024]{1,0:T(8,128)(2,1)S(1)}, u32[]{:S(2)}, u32[]{:S(2)}) collective-permute-start(f16[128,1024]{1,0:T(8,128)(2,1)S(1)} %multiply_convert_fusion.1), channel_id=1, source_target_pairs={{0,1},{3,2},{4,5},{7,6},{8,9},{11,10},{12,13},{15,14},{16,17},{19,... | collective-permute-start | bytes 786440 | tf_op jit(solution)/shard_map/cond/branch_0_fun/ppermute | solution.py:215
  103.7 13.2 %collective-permute-start.19 = (f16[128,1024]{1,0:T(8,128)(2,1)S(1)}, f16[128,1024]{1,0:T(8,128)(2,1)S(1)}, u32[]{:S(2)}, u32[]{:S(2)}) collective-permute-start(f16[128,1024]{1,0:T(8,128)(2,1)S(1)} %add_convert_fusion.4), channel_id=1, source_target_pairs={{1,2},{2,1},{5,6},{6,5},{9,10},{10,9},{13,14},{14,13},{17,18},{18,... | collective-permute-start | bytes 786440 | tf_op jit(solution)/shard_map/cond/branch_0_fun/ppermute | solution.py:222
  105.1 13.8 %collective-permute-start.20 = (f16[128,1024]{1,0:T(8,128)(2,1)S(1)}, f16[128,1024]{1,0:T(8,128)(2,1)S(1)}, u32[]{:S(2)}, u32[]{:S(2)}) collective-permute-start(f16[128,1024]{1,0:T(8,128)(2,1)S(1)} %add_convert_fusion.3), channel_id=1, source_target_pairs={{1,0},{2,3},{5,4},{6,7},{9,8},{10,11},{13,12},{14,15},{17,16},{18,... | collective-permute-start | bytes 786440 | tf_op jit(solution)/shard_map/cond/branch_0_fun/ppermute | solution.py:225
  110.9 16.8 %collective-permute-start.22 = (f16[128,512]{1,0:T(8,128)(2,1)S(1)}, f16[128,512]{1,0:T(8,128)(2,1)S(1)}, u32[]{:S(2)}, u32[]{:S(2)}) collective-permute-start(f16[128,512]{1,0:T(8,128)(2,1)S(1)} %multiply_convert_fusion.6), channel_id=1, source_target_pairs={{0,1},{3,2},{4,5},{7,6},{8,9},{11,10},{12,13},{15,14},{16,17},{19,... | collective-permute-start | bytes 393224 | tf_op jit(solution)/shard_map/cond/branch_0_fun/ppermute | solution.py:215
  116.2 12.8 %collective-permute-start.23 = (f16[128,1024]{1,0:T(8,128)(2,1)S(1)}, f16[128,1024]{1,0:T(8,128)(2,1)S(1)}, u32[]{:S(2)}, u32[]{:S(2)}) collective-permute-start(f16[128,1024]{1,0:T(8,128)(2,1)S(1)} %add_convert_fusion.2), channel_id=1, source_target_pairs={{1,2},{2,1},{5,6},{6,5},{9,10},{10,9},{13,14},{14,13},{17,18},{18,... | collective-permute-start | bytes 786440 | tf_op jit(solution)/shard_map/cond/branch_0_fun/ppermute | solution.py:222
  117.7 13.5 %collective-permute-start.24 = (f16[128,1024]{1,0:T(8,128)(2,1)S(1)}, f16[128,1024]{1,0:T(8,128)(2,1)S(1)}, u32[]{:S(2)}, u32[]{:S(2)}) collective-permute-start(f16[128,1024]{1,0:T(8,128)(2,1)S(1)} %add_convert_fusion.1), channel_id=1, source_target_pairs={{1,0},{2,3},{5,4},{6,7},{9,8},{10,11},{13,12},{14,15},{17,16},{18,... | collective-permute-start | bytes 786440 | tf_op jit(solution)/shard_map/cond/branch_0_fun/ppermute | solution.py:225
  122.6 12.2 %collective-permute-start.21 = (f16[128,512]{1,0:T(8,128)(2,1)S(1)}, f16[128,512]{1,0:T(8,128)(2,1)S(1)}, u32[]{:S(2)}, u32[]{:S(2)}) collective-permute-start(f16[128,512]{1,0:T(8,128)(2,1)S(1)} %multiply_convert_fusion.7), channel_id=1, source_target_pairs={{0,1},{3,2},{4,5},{7,6},{8,9},{11,10},{12,13},{15,14},{16,17},{19,... | collective-permute-start | bytes 393224 | tf_op jit(solution)/shard_map/cond/branch_0_fun/ppermute | solution.py:215
  187.4 29.7 %collective-permute-start.152 = (bf16[2,128,768]{2,1,0:T(8,128)(2,1)S(1)}, bf16[2,128,768]{2,1,0:T(8,128)(2,1)S(1)}, u32[]{:S(2)}, u32[]{:S(2)}) collective-permute-start(bf16[2,128,768]{2,1,0:T(8,128)(2,1)S(1)} %broadcast_select_fusion), channel_id=1, source_target_pairs={{0,4},{4,0},{8,12},{12,8},{1,5},{5,1},{9,13},{13,9},{2,6},{6,2},{1... | collective-permute-start | bytes 1179656 | tf_op jit(solution)/shard_map/ppermute | solution.py:22
  217.2 53.9 %collective-permute-start.153 = (bf16[1,128,768]{2,1,0:T(8,128)(2,1)S(1)}, bf16[1,128,768]{2,1,0:T(8,128)(2,1)S(1)}, u32[]{:S(2)}, u32[]{:S(2)}) collective-permute-start(bf16[1,128,768]{2,1,0:T(8,128)(2,1)S(1)} %select_bitcast_fusion.14), channel_id=1, source_target_pairs={{0,8},{4,12},{8,0},{12,4},{1,9},{5,13},{9,1},{13,5},{2,10},{6,14},... | collective-permute-start | bytes 589832 | tf_op jit(solution)/shard_map/ppermute | solution.py:22
  (20 other events, 173.8 us)

commit v2 on v1

v2 whole, which is shorter than its diff:
```python
import functools
import math

import jax
import jax.numpy as jnp
from jax import lax
from jax.experimental import pallas as pl
from jax.experimental.pallas import tpu as pltpu
from jax.sharding import PartitionSpec as P

BF, HALF, F32 = jnp.bfloat16, jnp.float16, jnp.float32
DONE = 3
BODY = 384
OUT, MID, BACK = [(0, 1), (3, 2)], [(1, 2), (2, 1)], [(1, 0), (2, 3)]
MIB = 1024 * 1024


def dot(a, b, dims=((1,), (0,))):
    return lax.dot_general(a, b, (dims, ((), ())), preferred_element_type=F32)


def then(value, after):
    return lax.optimization_barrier((value, after))[0]


def swap(value, axis, stride):
    n = lax.axis_size(axis)
    return lax.ppermute(value, axis, [(i, i ^ stride) for i in range(n)])


def gather_expert(value):
    n = lax.axis_size("expert")
    me = lax.axis_index("expert")
    held, stage, stride = value, 0, n // 2
    while stride >= 1:
        other = swap(held, "expert", stride)
        low = (me & stride) == 0
        held = jnp.stack([jnp.where(low, held, other), jnp.where(low, other, held)], axis=stage)
        stage, stride = stage + 1, stride // 2
    return held.reshape((n,) + value.shape)


def scatter_expert(value):
    n = lax.axis_size("expert")
    me = lax.axis_index("expert")
    stride = 1
    while stride < n:
        value = value.reshape((-1, 2) + value.shape[1:])
        low = (me & stride) == 0
        keep = jnp.where(low, value[:, 0], value[:, 1])
        send = jnp.where(low, value[:, 1], value[:, 0])
        got = swap(send, "expert", stride)
        value = (keep.astype(F32) + got.astype(F32)).astype(BF)
        stride *= 2
    return value[0]


def chunks_of(total, body):
    body = min(body, total // 2)
    sizes = [body] * (total // body) + ([total % body] if total % body else [])
    return [(sum(sizes[:i]), n) for i, n in enumerate(sizes)]


ANY = pl.BlockSpec(memory_space=pl.ANY)


def whole(shape):
    return pl.BlockSpec(shape, lambda i: (0,) * len(shape))


class Part:
    def __init__(self, at, n):
        self.at, self.n, self.wide = at, n, n if n % 256 else 256
        self.steps = n // self.wide

    def inside(self, height):
        first, steps = self.at // self.wide, self.steps
        return pl.BlockSpec((height, self.wide), lambda i: (0, first + jnp.minimum(i, steps - 1)))

    def own(self, height):
        steps = self.steps
        return pl.BlockSpec((height, 2 * self.wide), lambda i: (0, jnp.minimum(i, steps - 1)))


def call(body, steps, ins, in_specs, outs, out_specs, alias, scratch, vmem):
    return pl.pallas_call(
        body,
        grid=(steps,),
        in_specs=in_specs,
        out_specs=out_specs,
        out_shape=outs,
        scratch_shapes=scratch,
        input_output_aliases=alias,
        compiler_params=pltpu.CompilerParams(vmem_limit_bytes=vmem),
        cost_estimate=pl.CostEstimate(flops=1, bytes_accessed=1, transcendentals=0),
    )(*ins)


def produce_body(x_ref, wg_ref, wu_ref, p_ref):
    n = wg_ref.shape[1]
    p_ref[:, :n] = dot(x_ref[...], wg_ref[...])
    p_ref[:, n:] = dot(x_ref[...], wu_ref[...])


def finish_body(first, packed, x_ref, wg_ref, wu_ref, t_ref, *refs):
    n = wg_ref.shape[1]
    pick_ref = refs[0] if packed else None
    cot_ref, back_in = refs[packed : packed + 2]
    acted_ref, gg_ref, ug_ref, back_ref = refs[-4:]

    @pl.when(first)
    def _():
        back_ref[...] = back_in[...]

    pre_gate, pre_up = t_ref[:, :n], t_ref[:, n:]
    sig = jax.nn.sigmoid(pre_gate)
    silu_v = pre_gate * sig
    cf = dot(pick_ref[...], cot_ref[...]) if packed else cot_ref[...].astype(F32)
    gp = (cf * pre_up * sig * (1.0 + pre_gate * (1.0 - sig))).astype(BF)
    up = (cf * silu_v).astype(BF)
    acted = (silu_v * pre_up).astype(BF)
    acted_ref[...] = dot(pick_ref[...], acted, ((0,), (0,))).astype(BF) if packed else acted
    gg_ref[...] = dot(x_ref[...], gp, ((0,), (0,))).astype(BF)
    ug_ref[...] = dot(x_ref[...], up, ((0,), (0,))).astype(BF)
    back_ref[...] += dot(gp, wg_ref[...], ((1,), (1,))) + dot(up, wu_ref[...], ((1,), (1,)))


def main_call(x, wg, wu, make=None, end=None):
    rows, width = x.shape
    ins, in_specs = [x], [whole(x.shape)]
    outs, out_specs, alias, scratch = [], [], {}, []
    end_steps = make_steps = 0
    if end is not None:
        part, t, pick, cot, acted, gg, ug, back = end
        packed = int(pick is not None)
        end_steps = part.steps
        for arr, spec, into in (
            (wg, part.inside(width), None),
            (wu, part.inside(width), None),
            (t, part.own(rows), None),
            (pick, None if pick is None else whole(pick.shape), None),
            (cot, part.inside(cot.shape[0]), None),
            (back, whole(back.shape), 3),
            (acted, ANY, 0),
            (gg, ANY, 1),
            (ug, ANY, 2),
        ):
            if arr is None:
                continue
            if into is not None:
                alias[len(ins)] = into
            ins.append(arr)
            in_specs.append(spec)
        outs += [jax.ShapeDtypeStruct(v, BF) for v in (cot.shape, wg.shape, wg.shape)]
        outs += [jax.ShapeDtypeStruct(back.shape, F32)]
        out_specs += [part.inside(cot.shape[0]), part.inside(width), part.inside(width), whole(back.shape)]
    if make is not None:
        make_steps, n = make.steps, make.n
        ins += [wg, wu]
        in_specs += [make.inside(width)] * 2
        outs.append(jax.ShapeDtypeStruct((rows, 2 * n), F32))
        out_specs.append(make.own(rows))
    n_in = len(ins)

    def body(*refs):
        i, o = refs[:n_in], refs[n_in:]
        step = pl.program_id(0)
        if make is not None:

            @pl.when(step < make_steps)
            def _():
                produce_body(i[0], i[-2], i[-1], o[-1])

        if end is not None:

            @pl.when(step < end_steps)
            def _():
                finish_body(step == 0, packed, *i[: 6 + packed], *o[:4])

    return call(body, max(end_steps, make_steps), ins, in_specs, outs, out_specs, alias, scratch, 30 * MIB)


def pipeline(rows, cap, scale, tokens, hit, rank, wg, wu, cot):
    groups, per = hit.shape
    width, hidden = wg.shape
    count = jnp.sum(hit.astype(F32), axis=1)
    packed = rows < groups * cap
    first = jnp.cumsum(count) - count if packed else cap * jnp.arange(groups, dtype=F32)
    place = jnp.where(hit, first[:, None] + rank, -1.0).reshape(1, groups * per)
    row = jnp.arange(rows, dtype=F32)[:, None]
    take = (row == place).astype(BF)
    x = dot(take, tokens).astype(BF)
    pick = None
    if packed:
        slot = jnp.arange(cap, dtype=F32)[None, :]
        slot_row = jnp.where(slot < count[:, None], first[:, None] + slot, -1.0).reshape(1, groups * cap)
        pick = (row == slot_row).astype(BF)

    dp = lax.axis_index("dp")
    inner = (dp == 1) | (dp == 2)
    parts = [Part(at, n) for at, n in chunks_of(hidden, BODY if 2 * rows > groups * cap else 1024)]
    acted = gg = ug = None
    back = jnp.zeros((rows, width), F32)
    token = x
    p, a, q, b, t, c = {}, {}, {}, {}, {}, {}
    last = len(parts)

    def finish(j):
        nonlocal token, acted, gg, ug, back
        both = jnp.where(inner, t.pop(j), c.pop(j)).astype(F32) * (1.0 / scale)
        args = (parts[j], both, pick, cot, acted, gg, ug, back)
        acted, gg, ug, back = main_call(then(x, token), wg, wu, None, args)
        token = back

    def add(one, two):
        return (one.astype(F32) + two.astype(F32)).astype(HALF)

    def make(j):
        p[j] = (main_call(then(x, token), wg, wu, parts[j])[0] * scale).astype(HALF)

    def send(j):
        a[j] = lax.ppermute(then(p[j], token), "dp", OUT)

    for j in range(min(2, last)):
        make(j)
        send(j)
    for j in range(2, min(4, last)):
        make(j)
    for k in range(last + DONE):
        if k < last:
            q[k] = token = add(p.pop(k), then(a.pop(k), token))
            b[k] = lax.ppermute(q[k], "dp", MID)
        if k + 2 < last:
            send(k + 2)
        if 0 <= k - 1 < last:
            t[k - 1] = token = add(q.pop(k - 1), then(b.pop(k - 1), token))
            c[k - 1] = lax.ppermute(t[k - 1], "dp", BACK)
        for j in (2 * k + 4, 2 * k + 5):
            if j < last:
                make(j)
        if k >= DONE:
            finish(k - DONE)
    own = dot(take, back.astype(BF), ((0,), (0,))).astype(BF)
    return acted, gg, ug, own


def local(tokens, expert_ids, w_gate, w_up, cotangent):
    rows, width = tokens.shape
    experts = lax.axis_size("expert")
    cap = min(rows, 4 * rows // experts)
    wg, wu, cot = w_gate[0], w_up[0], cotangent[0]
    me = lax.axis_index("expert")
    bound = 6.0 * 0.109375 * width * lax.axis_size("dp")
    scale = 2.0 ** math.floor(math.log2(65000.0 / bound))
    ids = jnp.pad(expert_ids.astype(BF), ((0, 0), (0, 126)))
    held = gather_expert(jnp.concatenate([tokens, ids], axis=1))
    all_tokens, all_ids = held[:, :, :width], held[:, :, width : width + 2]
    hit = jnp.any(all_ids == me.astype(BF), axis=2)
    before = (jnp.arange(rows)[:, None] < jnp.arange(rows)[None, :]).astype(BF)
    rank = dot(hit.astype(BF), before)
    slots = experts * cap
    sizes = sorted({slots * part // 16 for part in (6, 8, 16)}, reverse=True)
    filled = jnp.sum(hit.astype(jnp.int32))
    which = jnp.sum((filled <= jnp.array(sizes[1:], jnp.int32)).astype(jnp.int32))
    acted, gg, ug, own = lax.switch(
        which,
        [functools.partial(pipeline, size, cap, scale) for size in sizes],
        all_tokens.reshape(experts * rows, width),
        hit,
        rank,
        wg,
        wu,
        cot,
    )
    part = scatter_expert(own.reshape(experts, rows, width))
    if lax.axis_size("section") == 2:
        total = part.astype(F32) + swap(part, "section", 1).astype(F32)
    else:
        total = lax.psum(part.astype(F32), "section")
    return acted[None], total.astype(BF), gg[None], ug[None]


def solution(mesh):
    placed = (
        P("expert", "dp"),
        P("expert", None),
        P("expert", "dp", "section"),
        P("expert", "dp", "section"),
        P("expert", None, "section"),
    )
    return jax.shard_map(
        local,
        mesh=mesh,
        in_specs=placed,
        out_specs=(
            P("expert", None, "section"),
            P("expert", "dp"),
            P("expert", "dp", "section"),
            P("expert", "dp", "section"),
        ),
        check_vma=False,
    )
```

time: 280 us -> 252 us (0.900)
  starting transfers between devices: 152 us -> 41.8 us
  waiting for transfers between devices: 27.3 us -> 133 us
  loops' own time: 27.5 us -> 13.3 us
  other arithmetic: 22.1 us -> 17.6 us
    ppermute x5, starting transfers between devices: 81.6 us -> 17.5 us  [swap(): return lax.ppermute(value, axis, [(i, i ^ stride) for i in range(n)])]
    ppermute x10 -> x4, waiting for transfers between devices: 0.03 us -> 54.7 us  [send(): a[j] = lax.ppermute(then(p[j], token), 'dp', OUT)]
    ppermute x10 -> x4, waiting for transfers between devices: 8.4 us -> 57 us  [pipeline(): c[k - 1] = lax.ppermute(t[k - 1], 'dp', BACK)]
    ppermute x10 -> x4, starting transfers between devices: 50.4 us -> 15.6 us  [send(): a[j] = lax.ppermute(then(p[j], token), 'dp', OUT)]
    another operation x1, loops' own time: 27.5 us -> 13.3 us  [local(): lax.switch(which, [functools.partial(pipeline, size, cap, scale) for size...]
    ppermute x10 -> x4, starting transfers between devices: 13.5 us -> 5.38 us  [pipeline(): c[k - 1] = lax.ppermute(t[k - 1], 'dp', BACK)]
    convert_element_type x32 -> x12, other arithmetic: 15 us -> 9.39 us  [the longest x8 5.87 us: add(): return (one.astype(F32) + two.astype(F32)).astype(HALF)]
    slice x11 -> x0, local copies, waits for them, and re-layouts: 5.64 us -> none  [the longest x10 5.13 us: pipeline(): q[k] = (p.pop(k) + a.pop(k).astype(F32) + token[0, 0]).astype(HALF)]
  transfers between devices with their start and end apart: 35 -> 17, of which waited for: 8 -> 11; matrix products, arithmetic and copies ran while one was open for 8% -> 4% of each run, Pallas kernels for 12% -> 7%
where the time goes in v2:
time: 252 us; the launch traced here: 251 us
  waiting for transfers between devices  133 us (53%)
  starting transfers between devices  41.8 us (17%)
  Pallas kernels  33.9 us (13%)
  other arithmetic  17.6 us (7%)
  loops' own time  13.3 us (5%)
  local copies, waits for them, and re-layouts  7.93 us (3%)
    ppermute x4, waiting for transfers between devices, pipeline(): c[k - 1] = lax.ppermute(t[k - 1], 'dp', BACK)  57 us
    ppermute x4, waiting for transfers between devices, send(): a[j] = lax.ppermute(then(p[j], token), 'dp', OUT)  54.7 us
    pallas_call x8, Pallas kernels, call(): pl.pallas_call(body, grid=(steps,), in_specs=in_specs, out_specs=out_spec...  33.9 us
    ppermute x5, waiting for transfers between devices, swap(): return lax.ppermute(value, axis, [(i, i ^ stride) for i in range(n)])  20.8 us
    ppermute x5, starting transfers between devices, swap(): return lax.ppermute(value, axis, [(i, i ^ stride) for i in range(n)])  17.5 us
    ppermute x4, starting transfers between devices, send(): a[j] = lax.ppermute(then(p[j], token), 'dp', OUT)  15.6 us
    another operation x1, loops' own time, local(): lax.switch(which, [functools.partial(pipeline, size, cap, scale) for size...  13.3 us
    convert_element_type x8, other arithmetic, add(): return (one.astype(F32) + two.astype(F32)).astype(HALF)  5.87 us
  transfers between devices with their start and end apart: 17, of which 11 were waited for; matrix products, arithmetic and copies ran while one was open for 4% of the time, Pallas kernels for 7%

profile of v2, /device:TPU:0, one launch (start us, length us, event | category | flops | bytes accessed | tf_op | source)
XLA Modules:
  0.0 250.8 jit_solution(12020853449329531255)
XLA Ops:
  2.4 3.0 %collective-permute-start.57 = (bf16[128,896]{1,0:T(8,128)(2,1)S(1)}, bf16[128,896]{1,0:T(8,128)(2,1)S(1)}, u32[]{:S(2)}, u32[]{:S(2)}) collective-permute-start(bf16[128,896]{1,0:T(8,128)(2,1)S(1)} %fusion.14), channel_id=1, source_target_pairs={{0,8},{4,12},{8,0},{12,4},{1,9},{5,13},{9,1},{13,5},{2,10},{6,14},... | collective-permute-start | bytes 688136 | tf_op jit(solution)/shard_map/ppermute | solution.py:28
  5.4 5.6 %collective-permute-done.57 = bf16[128,896]{1,0:T(8,128)(2,1)S(1)} collective-permute-done((bf16[128,896]{1,0:T(8,128)(2,1)S(1)}, bf16[128,896]{1,0:T(8,128)(2,1)S(1)}, u32[]{:S(2)}, u32[]{:S(2)}) %collective-permute-start.57) | collective-permute-done | bytes 229408 | tf_op jit(solution)/shard_map/ppermute | solution.py:28
  17.1 204.3 %conditional.1 = (bf16[512,4096]{1,0:T(8,128)(2,1)}, bf16[768,4096]{1,0:T(8,128)(2,1)}, bf16[768,4096]{1,0:T(8,128)(2,1)}, bf16[2,2,128,768]{3,2,1,0:T(8,128)(2,...) conditional(s32[]{:T(128)} %clamp.3, (f32[4,128]{1,0:T(4,128)S(1)}, ...), branch_computations={%region_3.4_spmd, %region_4.7_spmd, %region_7.10_spmd} | conditional | flops 869925888 | bytes 384068096 | solution.py:265
  25.4 4.5 %branch_1_fun.10 = f32[256,2048]{1,0:T(8,128)S(1)} custom-call(bf16[256,768]{1,0:T(8,128)(2,1)S(1)} %convolution_convert_fusion.3.refs_0_, bf16[768,4096]{1,0:T(8,128)(2,1)} %get-tuple-element.143.refs_1_, bf16[768,4096]{1,0:T(8,128)(2,1)} %get-tuple-element.144.refs_2_), custom_call_target="tpu_custom_call" | custom-call | flops 1 | bytes 1 | tf_op jit(solution)/shard_map/cond/branch_1_fun/pallas_call | solution.py:86
  31.6 4.7 %collective-permute-start.34 = (f16[256,2048]{1,0:T(8,128)(2,1)}, f16[256,2048]{1,0:T(8,128)(2,1)}, u32[]{:S(2)}, u32[]{:S(2)}) collective-permute-start(f16[256,2048]{1,0:T(8,128)(2,1)} %multiply_convert_fusion.12), channel_id=1, source_target_pairs={{0,1},{3,2},{4,5},{7,6},{8,9},{11,10},{12,13},{15,14},{16,17},{19,... | collective-permute-start | bytes 3145736 | tf_op jit(solution)/shard_map/cond/branch_1_fun/ppermute | solution.py:222
  36.3 2.2 branch_1_fun.9
  39.8 2.3 collective-permute-start.33
  42.1 2.2 branch_1_fun.11
  44.2 2.2 branch_1_fun.8
  48.5 5.9 %collective-permute-done.34 = f16[256,2048]{1,0:T(8,128)(2,1)} collective-permute-done((f16[256,2048]{1,0:T(8,128)(2,1)}, f16[256,2048]{1,0:T(8,128)(2,1)}, u32[]{:S(2)}, u32[]{:S(2)}) %collective-permute-start.34) | collective-permute-done | bytes 1048608 | tf_op jit(solution)/shard_map/cond/branch_1_fun/ppermute | solution.py:222
  57.1 19.6 %collective-permute-done.33 = f16[256,2048]{1,0:T(8,128)(2,1)} collective-permute-done((f16[256,2048]{1,0:T(8,128)(2,1)S(1)}, f16[256,2048]{1,0:T(8,128)(2,1)}, u32[]{:S(2)}, u32[]{:S(2)}) %collective-permute-start.33) | collective-permute-done | bytes 1048608 | tf_op jit(solution)/shard_map/cond/branch_1_fun/ppermute | solution.py:222
  76.8 4.5 %collective-permute-start.37 = (f16[256,2048]{1,0:T(8,128)(2,1)S(1)}, f16[256,2048]{1,0:T(8,128)(2,1)S(1)}, u32[]{:S(2)}, u32[]{:S(2)}) collective-permute-start(f16[256,2048]{1,0:T(8,128)(2,1)S(1)} %multiply_convert_fusion.11), channel_id=1, source_target_pairs={{0,1},{3,2},{4,5},{7,6},{8,9},{11,10},{12,13},{15,14},{16,17},{19,... | collective-permute-start | bytes 3145736 | tf_op jit(solution)/shard_map/cond/branch_1_fun/ppermute | solution.py:222
  83.9 4.0 %collective-permute-start.35 = (f16[256,2048]{1,0:T(8,128)(2,1)S(1)}, f16[256,2048]{1,0:T(8,128)(2,1)S(1)}, u32[]{:S(2)}, u32[]{:S(2)}) collective-permute-start(f16[256,2048]{1,0:T(8,128)(2,1)S(1)} %multiply_convert_fusion.14), channel_id=1, source_target_pairs={{0,1},{3,2},{4,5},{7,6},{8,9},{11,10},{12,13},{15,14},{16,17},{19,... | collective-permute-start | bytes 3145736 | tf_op jit(solution)/shard_map/cond/branch_1_fun/ppermute | solution.py:222
  89.7 10.3 %collective-permute-done.37 = f16[256,2048]{1,0:T(8,128)(2,1)S(1)} collective-permute-done((f16[256,2048]{1,0:T(8,128)(2,1)S(1)}, f16[256,2048]{1,0:T(8,128)(2,1)S(1)}, u32[]{:S(2)}, u32[]{:S(2)}) %collective-permute-start.37) | collective-permute-done | bytes 1048608 | tf_op jit(solution)/shard_map/cond/branch_1_fun/ppermute | solution.py:222
  102.9 18.8 %collective-permute-done.35 = f16[256,2048]{1,0:T(8,128)(2,1)S(1)} collective-permute-done((f16[256,2048]{1,0:T(8,128)(2,1)S(1)}, f16[256,2048]{1,0:T(8,128)(2,1)S(1)}, u32[]{:S(2)}, u32[]{:S(2)}) %collective-permute-start.35) | collective-permute-done | bytes 1048608 | tf_op jit(solution)/shard_map/cond/branch_1_fun/ppermute | solution.py:222
  125.9 6.5 %branch_1_fun.12 = (bf16[512,4096]{1,0:T(8,128)(2,1)}, bf16[768,4096]{1,0:T(8,128)(2,1)}, bf16[768,4096]{1,0:T(8,128)(2,1)}, f32[256,768]{1,0:T(8,128)S(1)}) custom-call(bf16[256,768]{1,0:T(8,128)(2,1)S(1)} %convolution_convert_fusion.3.refs_0_, bf16[768,4096]{1,0:T(8,128)(2,1)S(1)} %bitcast.66, ...), custom_call_target="tpu_custom_call", output_to_operand_aliasing={{3}: (6, {})} | custom-call | flops 1 | bytes 1 | tf_op jit(solution)/shard_map/cond/branch_1_fun/pallas_call | solution.py:86
  136.2 5.5 %branch_1_fun.13 = (bf16[512,4096]{1,0:T(8,128)(2,1)}, bf16[768,4096]{1,0:T(8,128)(2,1)}, bf16[768,4096]{1,0:T(8,128)(2,1)}, f32[256,768]{1,0:T(8,128)S(1)}) custom-call(bf16[256,768]{1,0:T(8,128)(2,1)S(1)} %convolution_convert_fusion.3.refs_0_, ...), custom_call_target="tpu_custom_call", output_to_operand_aliasing={{3}: (6, {}), {0}: (7, {}), {1}: (8, {}), {2}: (9, {})} | custom-call | flops 1 | bytes 1 | tf_op jit(solution)/shard_map/cond/branch_1_fun/pallas_call | solution.py:86
  141.7 34.6 %collective-permute-done.44 = f16[256,2048]{1,0:T(8,128)(2,1)S(1)} collective-permute-done((f16[256,2048]{1,0:T(8,128)(2,1)S(1)}, f16[256,2048]{1,0:T(8,128)(2,1)S(1)}, u32[]{:S(2)}, u32[]{:S(2)}) %collective-permute-start.44) | collective-permute-done | bytes 1048608 | tf_op jit(solution)/shard_map/cond/branch_1_fun/ppermute | solution.py:237
  176.2 22.5 %collective-permute-done.43 = f16[256,2048]{1,0:T(8,128)(2,1)S(1)} collective-permute-done((f16[256,2048]{1,0:T(8,128)(2,1)S(1)}, f16[256,2048]{1,0:T(8,128)(2,1)S(1)}, u32[]{:S(2)}, u32[]{:S(2)}) %collective-permute-start.43) | collective-permute-done | bytes 1048608 | tf_op jit(solution)/shard_map/cond/branch_1_fun/ppermute | solution.py:237
  199.7 5.5 %branch_1_fun.14 = (bf16[512,4096]{1,0:T(8,128)(2,1)}, bf16[768,4096]{1,0:T(8,128)(2,1)}, bf16[768,4096]{1,0:T(8,128)(2,1)}, f32[256,768]{1,0:T(8,128)S(1)}) custom-call(bf16[256,768]{1,0:T(8,128)(2,1)S(1)} %convolution_convert_fusion.3.refs_0_, ...), custom_call_target="tpu_custom_call", output_to_operand_aliasing={{3}: (6, {}), {0}: (7, {}), {1}: (8, {}), {2}: (9, {})} | custom-call | flops 1 | bytes 1 | tf_op jit(solution)/shard_map/cond/branch_1_fun/pallas_call | solution.py:86
  205.2 5.5 %branch_1_fun.15 = (bf16[512,4096]{1,0:T(8,128)(2,1)}, bf16[768,4096]{1,0:T(8,128)(2,1)}, bf16[768,4096]{1,0:T(8,128)(2,1)}, f32[256,768]{1,0:T(8,128)S(1)}) custom-call(bf16[256,768]{1,0:T(8,128)(2,1)S(1)} %convolution_convert_fusion.3.refs_0_, ...), custom_call_target="tpu_custom_call", output_to_operand_aliasing={{3}: (6, {}), {0}: (7, {}), {1}: (8, {}), {2}: (9, {})} | custom-call | flops 1 | bytes 1 | tf_op jit(solution)/shard_map/cond/branch_1_fun/pallas_call | solution.py:86
  221.5 12.8 %collective-permute-start.59 = (bf16[2,128,768]{2,1,0:T(8,128)(2,1)S(1)}, bf16[2,128,768]{2,1,0:T(8,128)(2,1)S(1)}, u32[]{:S(2)}, u32[]{:S(2)}) collective-permute-start(bf16[2,128,768]{2,1,0:T(8,128)(2,1)S(1)} %broadcast_select_fusion), channel_id=1, source_target_pairs={{0,4},{4,0},{8,12},{12,8},{1,5},{5,1},{9,13},{13,9},{2,6},{6,2},{1... | collective-permute-start | bytes 1179656 | tf_op jit(solution)/shard_map/ppermute | solution.py:28
  235.9 7.2 %collective-permute-done.60 = bf16[1,128,768]{2,1,0:T(8,128)(2,1)S(1)} collective-permute-done((bf16[1,128,768]{2,1,0:T(8,128)(2,1)S(1)}, bf16[1,128,768]{2,1,0:T(8,128)(2,1)S(1)}, u32[]{:S(2)}, u32[]{:S(2)}) %collective-permute-start.60) | collective-permute-done | bytes 196640 | tf_op jit(solution)/shard_map/ppermute | solution.py:28
  244.7 4.9 %collective-permute-done.61 = bf16[128,768]{1,0:T(8,128)(2,1)S(1)} collective-permute-done((bf16[128,768]{1,0:T(8,128)(2,1)S(1)}, bf16[128,768]{1,0:T(8,128)(2,1)S(1)}, u32[]{:S(2)}, u32[]{:S(2)}) %collective-permute-start.61) | collective-permute-done | bytes 196640 | tf_op jit(solution)/shard_map/ppermute | solution.py:28
  (98 shorter events, 40.9 us)
Async XLA Ops:
  2.4 8.6 %collective-permute-start.57 = (bf16[128,896]{1,0:T(8,128)(2,1)S(1)}, bf16[128,896]{1,0:T(8,128)(2,1)S(1)}, u32[]{:S(2)}, u32[]{:S(2)}) collective-permute-start(bf16[128,896]{1,0:T(8,128)(2,1)S(1)} %fusion.14), channel_id=1, source_target_pairs={{0,8},{4,12},{8,0},{12,4},{1,9},{5,13},{9,1},{13,5},{2,10},{6,14},... | collective-permute-start | bytes 688136 | tf_op jit(solution)/shard_map/ppermute | solution.py:28
  12.1 1.9 collective-permute-start.58
  25.4 10.9 %slice-start.4 = ((s8[6291456]{0:T(1024)(128)(4,1)}), s8[4194304]{0:T(1024)(128)(4,1)S(1)}, s32[]{:S(2)}) async-start(s8[6291456]{0:T(1024)(128)(4,1)} %bitcast.63), calls=%async_computation.4 | async-start | bytes 8388608 | tf_op jit(solution)/shard_map/cond
  25.4 10.9 %slice-start.16 = ((s8[6291456]{0:T(1024)(128)(4,1)}), s8[4194304]{0:T(1024)(128)(4,1)S(1)}, s32[]{:S(2)}) async-start(s8[6291456]{0:T(1024)(128)(4,1)} %bitcast.78), calls=%async_computation.16 | async-start | bytes 8388608 | tf_op jit(solution)/shard_map/cond
  25.4 10.9 %slice-start.5 = ((s8[6291456]{0:T(1024)(128)(4,1)}), s8[2097152]{0:T(1024)(128)(4,1)S(1)}, s32[]{:S(2)}) async-start(s8[6291456]{0:T(1024)(128)(4,1)} %bitcast.63), calls=%async_computation.5 | async-start | bytes 4194304 | tf_op jit(solution)/shard_map/cond
  25.4 10.9 %slice-start.17 = ((s8[6291456]{0:T(1024)(128)(4,1)}), s8[2097152]{0:T(1024)(128)(4,1)S(1)}, s32[]{:S(2)}) async-start(s8[6291456]{0:T(1024)(128)(4,1)} %bitcast.78), calls=%async_computation.17 | async-start | bytes 4194304 | tf_op jit(solution)/shard_map/cond
  31.6 22.8 %collective-permute-start.34 = (f16[256,2048]{1,0:T(8,128)(2,1)}, f16[256,2048]{1,0:T(8,128)(2,1)}, u32[]{:S(2)}, u32[]{:S(2)}) collective-permute-start(f16[256,2048]{1,0:T(8,128)(2,1)} %multiply_convert_fusion.12), channel_id=1, source_target_pairs={{0,1},{3,2},{4,5},{7,6},{8,9},{11,10},{12,13},{15,14},{16,17},{19,... | collective-permute-start | bytes 3145736 | tf_op jit(solution)/shard_map/cond/branch_1_fun/ppermute | solution.py:222
  39.8 37.0 %collective-permute-start.33 = (f16[256,2048]{1,0:T(8,128)(2,1)S(1)}, f16[256,2048]{1,0:T(8,128)(2,1)}, u32[]{:S(2)}, u32[]{:S(2)}) collective-permute-start(f16[256,2048]{1,0:T(8,128)(2,1)S(1)} %multiply_convert_fusion.13), channel_id=1, source_target_pairs={{0,1},{3,2},{4,5},{7,6},{8,9},{11,10},{12,13},{15,14},{16,17},{19,... | collective-permute-start | bytes 3145736 | tf_op jit(solution)/shard_map/cond/branch_1_fun/ppermute | solution.py:222
  56.0 25.3 %copy-start.3 = (f32[256,2048]{1,0:T(8,128)S(1)}, f32[256,2048]{1,0:T(8,128)}, u32[]{:S(2)}) copy-start(f32[256,2048]{1,0:T(8,128)} %copy-done.2) | copy-start | bytes 6291460 | tf_op jit(solution)/shard_map/cond
  56.1 31.9 %collective-permute-start.38 = (f16[256,2048]{1,0:T(8,128)(2,1)S(1)}, f16[256,2048]{1,0:T(8,128)(2,1)S(1)}, u32[]{:S(2)}, u32[]{:S(2)}) collective-permute-start(f16[256,2048]{1,0:T(8,128)(2,1)S(1)} %add_convert_fusion.29), channel_id=1, source_target_pairs={{1,2},{2,1},{5,6},{6,5},{9,10},{10,9},{13,14},{14,13},{17,18},{18,... | collective-permute-start | bytes 3145736 | tf_op jit(solution)/shard_map/cond/branch_1_fun/ppermute | solution.py:232
  76.8 23.2 %collective-permute-start.37 = (f16[256,2048]{1,0:T(8,128)(2,1)S(1)}, f16[256,2048]{1,0:T(8,128)(2,1)S(1)}, u32[]{:S(2)}, u32[]{:S(2)}) collective-permute-start(f16[256,2048]{1,0:T(8,128)(2,1)S(1)} %multiply_convert_fusion.11), channel_id=1, source_target_pairs={{0,1},{3,2},{4,5},{7,6},{8,9},{11,10},{12,13},{15,14},{16,17},{19,... | collective-permute-start | bytes 3145736 | tf_op jit(solution)/shard_map/cond/branch_1_fun/ppermute | solution.py:222
  83.0 17.0 %copy-start.1 = (f32[256,2048]{1,0:T(8,128)S(1)}, f32[256,2048]{1,0:T(8,128)}, u32[]{:S(2)}) copy-start(f32[256,2048]{1,0:T(8,128)} %copy-done) | copy-start | bytes 6291460 | tf_op jit(solution)/shard_map/cond
  83.0 18.2 %collective-permute-start.36 = (f16[256,2048]{1,0:T(8,128)(2,1)S(1)}, f16[256,2048]{1,0:T(8,128)(2,1)S(1)}, u32[]{:S(2)}, u32[]{:S(2)}) collective-permute-start(f16[256,2048]{1,0:T(8,128)(2,1)S(1)} %add_convert_fusion.28), channel_id=1, source_target_pairs={{1,2},{2,1},{5,6},{6,5},{9,10},{10,9},{13,14},{14,13},{17,18},{18,... | collective-permute-start | bytes 3145736 | tf_op jit(solution)/shard_map/cond/branch_1_fun/ppermute | solution.py:232
  83.9 37.8 %collective-permute-start.35 = (f16[256,2048]{1,0:T(8,128)(2,1)S(1)}, f16[256,2048]{1,0:T(8,128)(2,1)S(1)}, u32[]{:S(2)}, u32[]{:S(2)}) collective-permute-start(f16[256,2048]{1,0:T(8,128)(2,1)S(1)} %multiply_convert_fusion.14), channel_id=1, source_target_pairs={{0,1},{3,2},{4,5},{7,6},{8,9},{11,10},{12,13},{15,14},{16,17},{19,... | collective-permute-start | bytes 3145736 | tf_op jit(solution)/shard_map/cond/branch_1_fun/ppermute | solution.py:222
  88.4 34.6 %collective-permute-start.41 = (f16[256,2048]{1,0:T(8,128)(2,1)S(1)}, f16[256,2048]{1,0:T(8,128)(2,1)S(1)}, u32[]{:S(2)}, u32[]{:S(2)}) collective-permute-start(f16[256,2048]{1,0:T(8,128)(2,1)S(1)} %add_convert_fusion.27), channel_id=1, source_target_pairs={{1,0},{2,3},{5,4},{6,7},{9,8},{10,11},{13,12},{14,15},{17,16},{18,... | collective-permute-start | bytes 3145736 | tf_op jit(solution)/shard_map/cond/branch_1_fun/ppermute | solution.py:237
  100.4 22.5 %collective-permute-start.40 = (f16[256,2048]{1,0:T(8,128)(2,1)S(1)}, f16[256,2048]{1,0:T(8,128)(2,1)S(1)}, u32[]{:S(2)}, u32[]{:S(2)}) collective-permute-start(f16[256,2048]{1,0:T(8,128)(2,1)S(1)} %add_convert_fusion.26), channel_id=1, source_target_pairs={{1,2},{2,1},{5,6},{6,5},{9,10},{10,9},{13,14},{14,13},{17,18},{18,... | collective-permute-start | bytes 3145736 | tf_op jit(solution)/shard_map/cond/branch_1_fun/ppermute | solution.py:232
  101.6 34.1 %collective-permute-start.42 = (f16[256,2048]{1,0:T(8,128)(2,1)S(1)}, f16[256,2048]{1,0:T(8,128)(2,1)S(1)}, u32[]{:S(2)}, u32[]{:S(2)}) collective-permute-start(f16[256,2048]{1,0:T(8,128)(2,1)S(1)} %add_convert_fusion.25), channel_id=1, source_target_pairs={{1,0},{2,3},{5,4},{6,7},{9,8},{10,11},{13,12},{14,15},{17,16},{18,... | collective-permute-start | bytes 3145736 | tf_op jit(solution)/shard_map/cond/branch_1_fun/ppermute | solution.py:237
  122.1 10.4 %collective-permute-start.39 = (f16[256,2048]{1,0:T(8,128)(2,1)S(1)}, f16[256,2048]{1,0:T(8,128)(2,1)S(1)}, u32[]{:S(2)}, u32[]{:S(2)}) collective-permute-start(f16[256,2048]{1,0:T(8,128)(2,1)S(1)} %add_convert_fusion.24), channel_id=1, source_target_pairs={{1,2},{2,1},{5,6},{6,5},{9,10},{10,9},{13,14},{14,13},{17,18},{18,... | collective-permute-start | bytes 3145736 | tf_op jit(solution)/shard_map/cond/branch_1_fun/ppermute | solution.py:232
  123.9 12.3 %slice-start.18 = ((s8[6291456]{0:T(1024)(128)(4,1)}), s8[4194304]{0:T(1024)(128)(4,1)S(1)}, s32[]{:S(2)}) async-start(s8[6291456]{0:T(1024)(128)(4,1)} %bitcast.80), calls=%async_computation.18 | async-start | bytes 8388608 | tf_op jit(solution)/shard_map/cond
  132.9 43.3 %collective-permute-start.44 = (f16[256,2048]{1,0:T(8,128)(2,1)S(1)}, f16[256,2048]{1,0:T(8,128)(2,1)S(1)}, u32[]{:S(2)}, u32[]{:S(2)}) collective-permute-start(f16[256,2048]{1,0:T(8,128)(2,1)S(1)} %add_convert_fusion.22), channel_id=1, source_target_pairs={{1,0},{2,3},{5,4},{6,7},{9,8},{10,11},{13,12},{14,15},{17,16},{18,... | collective-permute-start | bytes 3145736 | tf_op jit(solution)/shard_map/cond/branch_1_fun/ppermute | solution.py:237
  134.2 64.5 %collective-permute-start.43 = (f16[256,2048]{1,0:T(8,128)(2,1)S(1)}, f16[256,2048]{1,0:T(8,128)(2,1)S(1)}, u32[]{:S(2)}, u32[]{:S(2)}) collective-permute-start(f16[256,2048]{1,0:T(8,128)(2,1)S(1)} %add_convert_fusion.23), channel_id=1, source_target_pairs={{1,0},{2,3},{5,4},{6,7},{9,8},{10,11},{13,12},{14,15},{17,16},{18,... | collective-permute-start | bytes 3145736 | tf_op jit(solution)/shard_map/cond/branch_1_fun/ppermute | solution.py:237
  221.5 14.1 %collective-permute-start.59 = (bf16[2,128,768]{2,1,0:T(8,128)(2,1)S(1)}, bf16[2,128,768]{2,1,0:T(8,128)(2,1)S(1)}, u32[]{:S(2)}, u32[]{:S(2)}) collective-permute-start(bf16[2,128,768]{2,1,0:T(8,128)(2,1)S(1)} %broadcast_select_fusion), channel_id=1, source_target_pairs={{0,4},{4,0},{8,12},{12,8},{1,5},{5,1},{9,13},{13,9},{2,6},{6,2},{1... | collective-permute-start | bytes 1179656 | tf_op jit(solution)/shard_map/ppermute | solution.py:28
  235.8 7.2 %collective-permute-start.60 = (bf16[1,128,768]{2,1,0:T(8,128)(2,1)S(1)}, bf16[1,128,768]{2,1,0:T(8,128)(2,1)S(1)}, u32[]{:S(2)}, u32[]{:S(2)}) collective-permute-start(bf16[1,128,768]{2,1,0:T(8,128)(2,1)S(1)} %select_bitcast_fusion.9), channel_id=1, source_target_pairs={{0,8},{4,12},{8,0},{12,4},{1,9},{5,13},{9,1},{13,5},{2,10},{6,14},... | collective-permute-start | bytes 589832 | tf_op jit(solution)/shard_map/ppermute | solution.py:28
  243.1 6.4 %collective-permute-start.61 = (bf16[128,768]{1,0:T(8,128)(2,1)S(1)}, bf16[128,768]{1,0:T(8,128)(2,1)S(1)}, u32[]{:S(2)}, u32[]{:S(2)}) collective-permute-start(bf16[128,768]{1,0:T(8,128)(2,1)S(1)} %fusion.15), channel_id=1, source_target_pairs={{0,16},{16,0},{1,17},{17,1},{2,18},{18,2},{3,19},{19,3},{4,20},{20... | collective-permute-start | bytes 589832 | tf_op jit(solution)/shard_map/ppermute | solution.py:28
  (9 other events, 32.3 us)
